TPU v7x, 32 devices: a whole 2x2x4 slice. The times are simulated.
32 devices in a mesh: owner: 16 (over z, y, x), pair: 2 (over core).
Axes of the slice: x: 2, y: 2, z: 4, core: 2. Of those that a mesh axis runs over, the one named last changes fastest.
Arguments:
- incident: float32 [32, 2, 32, 512], P('owner', None, None, 'pair'), may hold values from -6 to 6
- tmat: float32 [32, 2, 512, 512], P('owner', None, 'pair'), may hold values from -0.1875 to 0.1875
- blocks: float32 [336, 2, 512, 512], P('owner', None, None, 'pair'), may hold values from -0.09375 to 0.09375
- block_rows: int32 [336], P('owner'), may hold values from 0 to 1
- partners: int32 [336], replicated, may hold values from 0 to 31, as said below
- live: int32 [16], P('owner'), may hold values from 1 to 21, as said below
- owner_of: int32 [32], replicated, may hold values from 0 to 31, as said below
Outputs:
- scattered: float32 [32, 2, 32, 512], P('owner', None, None, 'pair')
- exciting: float32 [32, 2, 32, 512], P('owner', None, None, 'pair')
Inputs may be any that keep to these rules, and one draw needn't show every extreme that they name: A permutation: particle p's coefficients and T-matrix stand in row owner_of[p]. `partners`: the 21 slots of one owner name distinct particles whose rows lie with owners either less than 7 positions away on either side around the cycle of owners or exactly 8 positions away, never the owner itself, at most 2 with any one other owner; for every owner some other owner holds exactly 2 of them. Slots n with n mod 21 below live[n // 21] are live; some owner has all 21 slots live.
All inputs are finite; a program needn't handle non-finite values.
Results may differ from a plain program's by a relative error of at most 0.0003.
Values sent between devices are 32-bit elements; how exact they have to be, the bound alone decides.
No kernel may reach another device: no remote copies, remote signals or barrier semaphores. Data moves between devices by JAX's collectives and lax.ppermute only.
A program may use at most 128 MiB of HBM per device.

v0:
```python
import jax
import jax.numpy as jnp
from jax import lax
from jax.sharding import PartitionSpec as P

ITERS = 2


HIGHEST = lax.Precision.HIGHEST


def from_behind(value, axis, steps):
    count = lax.axis_size(axis)
    pairs = [(source, (source + steps) % count) for source in range(count)]
    return lax.ppermute(value, axis, pairs)


def complex_rows(matrix, vectors):
    directions = vectors.shape[1]
    stacked = vectors.reshape(2 * directions, vectors.shape[2])
    real_part = jnp.einsum(
        "km,lm->kl", stacked, matrix[0], precision=HIGHEST, preferred_element_type=jnp.float32
    )
    imag_part = jnp.einsum(
        "km,lm->kl", stacked, matrix[1], precision=HIGHEST, preferred_element_type=jnp.float32
    )
    return jnp.stack(
        (
            real_part[:directions] - imag_part[directions:],
            imag_part[:directions] + real_part[directions:],
        )
    )


def complex_cols(matrix, vectors):
    directions = vectors.shape[1]
    stacked = vectors.reshape(2 * directions, vectors.shape[2])
    real_part = jnp.einsum(
        "kl,lm->km", stacked, matrix[0], precision=HIGHEST, preferred_element_type=jnp.float32
    )
    imag_part = jnp.einsum(
        "kl,lm->km", stacked, matrix[1], precision=HIGHEST, preferred_element_type=jnp.float32
    )
    return jnp.stack(
        (
            real_part[:directions] - imag_part[directions:],
            imag_part[:directions] + real_part[directions:],
        )
    )


def gather_field(field_half):
    return lax.all_gather(field_half, "pair", axis=3, tiled=True)


def local(incident, tmat, blocks, block_rows, partners, live, owner_of):
    particles = incident.shape[0]
    directions = incident.shape[2]
    half_width = incident.shape[3]
    block_count = blocks.shape[0]
    owners = lax.axis_size("owner")
    my_owner = lax.axis_index("owner")
    particle_ids = jnp.arange(owner_of.shape[0], dtype=jnp.int32)
    every_row = jnp.sum(
        jnp.where(partners[:, None] == particle_ids[None, :], owner_of[None, :], 0), axis=1
    )
    partner_row = lax.dynamic_slice_in_dim(every_row, my_owner * block_count, block_count)
    alive_count = live[0]
    apply_tmat = jax.vmap(complex_rows)

    def coefficients(field_full):
        return (apply_tmat(tmat, field_full), None)

    window_reach = min(8, (owners - 1) // 2)
    group_total = 2 * window_reach - 1
    capacity = (block_count + group_total - 1) // group_total
    distances = (
        [owners // 2]
        + list(range(1, window_reach))
        + [-step_size for step_size in range(1, window_reach)]
    )
    partner_owner = partner_row // particles
    gap_owner = (partner_owner - my_owner) % owners
    group_index = jnp.where(
        gap_owner == owners // 2,
        0,
        jnp.where(gap_owner < window_reach, gap_owner, window_reach + owners - gap_owner - 1),
    )
    positions = jnp.arange(block_count, dtype=jnp.int32)
    earlier = (group_index[:, None] == group_index[None, :]) & (
        positions[None, :] < positions[:, None]
    )
    rank_own = jnp.sum(earlier.astype(jnp.int32), axis=1)
    landing = group_index * capacity + rank_own
    holders = (my_owner - jnp.array(distances, dtype=jnp.int32)) % owners
    owner_grid = (every_row // particles).reshape(owners, block_count)
    local_grid = (every_row % particles).reshape(owners, block_count)
    holder_pick = (holders[:, None] == jnp.arange(owners, dtype=jnp.int32)[None, :]).astype(
        jnp.int32
    )
    their_owner = jnp.sum(holder_pick[:, :, None] * owner_grid[None, :, :], axis=1)
    their_local = jnp.sum(holder_pick[:, :, None] * local_grid[None, :, :], axis=1)
    matched = their_owner == my_owner
    match_rank = jnp.cumsum(matched.astype(jnp.int32), axis=1) - 1
    rank_ids = jnp.arange(capacity, dtype=jnp.int32)
    hit = matched[:, :, None] & (match_rank[:, :, None] == rank_ids[None, None, :])
    send_rows = jnp.sum(jnp.where(hit, their_local[:, :, None] + 1, 0), axis=1) - 1
    half_coeff, whole_coeff = coefficients(gather_field(incident))
    exciting = incident
    for iteration in range(ITERS):
        full_coeff = lax.all_gather(half_coeff, "pair", axis=3, tiled=True)
        pieces = []
        for fetch_group_number, fetch_distance in enumerate(distances):
            row_pick = send_rows[fetch_group_number]
            outbound = jnp.where(
                (row_pick >= 0)[:, None, None, None],
                half_coeff[jnp.clip(row_pick, 0, particles - 1)],
                0.0,
            )
            pieces.append(from_behind(outbound, "owner", -fetch_distance))
        arrived = jnp.concatenate(pieces, axis=0)
        fetched = arrived[landing]

        def apply_block(block_index, totals):
            near_acc, given_back = totals
            one_block = lax.dynamic_index_in_dim(blocks, block_index, 0, keepdims=False)
            holder_row = block_rows[block_index]
            forward = complex_rows(one_block, fetched[block_index])
            near_acc = near_acc.at[holder_row].add(forward)
            backward = complex_cols(one_block, full_coeff[holder_row])
            given_back = given_back.at[block_index].set(backward)
            return (near_acc, given_back)

        start_near = jnp.zeros((particles, 2, directions, full_coeff.shape[3]), jnp.float32)
        start_back = jnp.zeros((block_count, 2, directions, half_width), jnp.float32)
        near_acc, given_back = lax.fori_loop(0, alive_count, apply_block, (start_near, start_back))
        near_field = lax.psum_scatter(near_acc, "pair", scatter_dimension=3, tiled=True)
        outgoing = (
            jnp.zeros((group_total * capacity, 2, directions, half_width), jnp.float32)
            .at[landing]
            .set(given_back)
        )
        incoming_list = []
        for group_number, distance in enumerate(distances):
            segment = outgoing[group_number * capacity : (group_number + 1) * capacity]
            incoming_list.append(from_behind(segment, "owner", distance))
        incoming = jnp.concatenate(incoming_list, axis=0)
        chosen = (
            send_rows.reshape(-1)[None, :] == jnp.arange(particles, dtype=jnp.int32)[:, None]
        ).astype(jnp.float32)
        summed = jnp.dot(
            chosen,
            incoming.reshape(group_total * capacity, -1),
            precision=HIGHEST,
            preferred_element_type=jnp.float32,
        )
        returned = summed.reshape(particles, 2, directions, half_width)
        exciting = incident + near_field + returned
        half_coeff, whole_coeff = coefficients(gather_field(exciting))
    return (half_coeff, exciting)


def solution(mesh):
    in_specs = (
        P("owner", None, None, "pair"),
        P("owner", None, "pair", None),
        P("owner", None, None, "pair"),
        P("owner"),
        P(),
        P("owner"),
        P(),
    )
    out_specs = (P("owner", None, None, "pair"), P("owner", None, None, "pair"))
    return jax.shard_map(local, mesh=mesh, in_specs=in_specs, out_specs=out_specs, check_vma=False)
```

profile of v0, /device:TPU:0, one launch (start us, length us, event | category | flops | bytes accessed | tf_op | source)
XLA Modules:
  0.0 901.9 jit_solution(1546476059121965493)
XLA Ops:
  16.2 4.0 collective-permute-start
  21.5 3.2 collective-permute-start.1
  50.1 3.8 collective-permute-start.10
  53.9 11.0 %collective-permute-done.6 = f32[2,2,32,256]{3,2,1,0:T(8,128)S(1)} collective-permute-done((f32[2,2,32,256]{3,2,1,0:T(8,128)}, f32[2,2,32,256]{3,2,1,0:T(8,128)S(1)}, u32[]{:S(2)}, u32[]{:S(2)}) %collective-permute-start.6) | collective-permute-done | bytes 131104 | tf_op jit(solution)/shard_map/ppermute | solution.py:15
  65.1 8.5 collective-permute-done.11
  75.7 274.0 %while.28 = (s32[]{:T(128)}, f32[2,2,32,512]{3,2,1,0:T(8,128)S(1)}, f32[21,2,32,256]{3,2,1,0:T(8,128)S(1)}, s32[]{:T(128)}, s32[21]{0:T(128)S(1)}, /*index=5*/f3...) while((s32[]{:T(128)}, f32[2,2,32,512]{3,2,1,0:T(8,128)S(1)}, ...), condition=%wide.region_9.10_spmd, body=%wide.region_6.9_spmd.sunk | while | flops 402833472 | bytes 4458809 | solution.py:136
  352.8 5.8 collective-permute-start.17
  358.6 13.7 %copy.73 = f32[2,2,32,512]{0,2,1,3:T(8,128)} copy(f32[2,2,32,512]{3,2,1,0:T(8,128)S(1)} %get-tuple-element.138) | data formatting | bytes 524288
  372.3 13.1 %reshape.907 = f32[512,128]{1,0:T(8,128)} reshape(f32[512,2,32,2]{3,2,1,0:T(8,128)} %bitcast.307) | data formatting | bytes 524288
  389.2 4.2 collective-permute-start.20
  409.8 10.5 %reshape.908 = f32[256,2,32,2]{3,2,1,0:T(8,128)} reshape(f32[256,128]{1,0:T(8,128)} %reduce-scatter.7.cloned.1.call-done) | data formatting | bytes 262144
  420.4 6.4 copy.74
  426.8 3.3 fusion.34
  449.3 6.6 collective-permute-start.26
  457.0 2.9 collective-permute-start.27
  463.0 3.3 collective-permute-start.29
  470.4 3.8 collective-permute-start.32
  474.9 10.1 %collective-permute-start.33 = (f32[2,2,32,256]{3,2,1,0:T(8,128)S(1)}, f32[2,2,32,256]{3,2,1,0:T(8,128)S(1)}, u32[]{:S(2)}, u32[]{:S(2)}) collective-permute-start(f32[2,2,32,256]{3,2,1,0:T(8,128)S(1)} %broadcast_select_fusion.5), channel_id=1, source_target_pairs={{0,2},{2,4},{4,6},{6,8},{8,10},{10,12},{12,14},{14,16},{16,18},{18... | collective-permute-start | bytes 393224 | tf_op jit(solution)/shard_map/ppermute | solution.py:15
  487.0 3.5 collective-permute-start.36
  492.0 4.1 collective-permute-start.38
  498.8 4.5 collective-permute-done.37
  504.6 3.2 gather_fusion.27
  509.1 288.4 %while.29 = (s32[]{:T(128)}, f32[2,2,32,512]{3,2,1,0:T(8,128)S(1)}, f32[21,2,32,256]{3,2,1,0:T(8,128)}, s32[]{:T(128)}, s32[21]{0:T(128)S(1)}, /*index=5*/f32[21...) while((s32[]{:T(128)}, f32[2,2,32,512]{3,2,1,0:T(8,128)S(1)}, ...), condition=%wide.region_15.16_spmd, body=%wide.region_12.15_spmd.sunk | while | flops 402833472 | bytes 4459828 | solution.py:136
  798.9 5.7 scatter_fusion.1
  807.4 5.6 collective-permute-start.43
  813.1 13.7 %copy.75 = f32[2,2,32,512]{0,2,1,3:T(8,128)} copy(f32[2,2,32,512]{3,2,1,0:T(8,128)S(1)} %get-tuple-element.140) | data formatting | bytes 524288
  826.8 13.1 %reshape.909 = f32[512,128]{1,0:T(8,128)} reshape(f32[512,2,32,2]{3,2,1,0:T(8,128)} %bitcast.308) | data formatting | bytes 524288
  843.8 4.2 collective-permute-start.46
  857.6 7.8 collective-permute-start.51
  869.4 10.5 %reshape.910 = f32[256,2,32,2]{3,2,1,0:T(8,128)} reshape(f32[256,128]{1,0:T(8,128)} %reduce-scatter.9.cloned.1.call-done) | data formatting | bytes 262144
  880.0 6.4 copy.76
  886.3 3.1 fusion.37
  (834 shorter events, 573.8 us)
Async XLA Ops:
  7.2 402.6 %reduce-scatter.7.cloned.1.call-start = ((), (), s32[]{:S(2)}) async-start(), calls=%async_computation.2 | async-start | bytes 393216
  16.2 25.9 %collective-permute-start = (f32[2,2,32,256]{3,2,1,0:T(8,128)S(1)}, f32[2,2,32,256]{3,2,1,0:T(8,128)S(1)}, u32[]{:S(2)}, u32[]{:S(2)}) collective-permute-start(f32[2,2,32,256]{3,2,1,0:T(8,128)S(1)} %broadcast_select_fusion.25), channel_id=1, source_target_pairs={{0,16},{2,18},{4,20},{6,22},{8,24},{10,26},{12,28},{14,30},{16,0},... | collective-permute-start | bytes 393224 | tf_op jit(solution)/shard_map/ppermute | solution.py:15
  21.5 21.9 %collective-permute-start.1 = (f32[2,2,32,256]{3,2,1,0:T(8,128)}, f32[2,2,32,256]{3,2,1,0:T(8,128)S(1)}, u32[]{:S(2)}, u32[]{:S(2)}) collective-permute-start(f32[2,2,32,256]{3,2,1,0:T(8,128)} %broadcast_select_fusion.24), channel_id=1, source_target_pairs={{0,30},{2,0},{4,2},{6,4},{8,6},{10,8},{12,10},{14,12},{16,14},{18,... | collective-permute-start | bytes 393224 | tf_op jit(solution)/shard_map/ppermute | solution.py:15
  26.0 19.7 %collective-permute-start.2 = (f32[2,2,32,256]{3,2,1,0:T(8,128)}, f32[2,2,32,256]{3,2,1,0:T(8,128)S(1)}, u32[]{:S(2)}, u32[]{:S(2)}) collective-permute-start(f32[2,2,32,256]{3,2,1,0:T(8,128)} %broadcast_select_fusion.23), channel_id=1, source_target_pairs={{0,28},{2,30},{4,0},{6,2},{8,4},{10,6},{12,8},{14,10},{16,12},{18,... | collective-permute-start | bytes 393224 | tf_op jit(solution)/shard_map/ppermute | solution.py:15
  27.2 18.6 %collective-permute-start.3 = (f32[2,2,32,256]{3,2,1,0:T(8,128)S(1)}, f32[2,2,32,256]{3,2,1,0:T(8,128)S(1)}, u32[]{:S(2)}, u32[]{:S(2)}) collective-permute-start(f32[2,2,32,256]{3,2,1,0:T(8,128)S(1)} %broadcast_select_fusion.22), channel_id=1, source_target_pairs={{0,26},{2,28},{4,30},{6,0},{8,2},{10,4},{12,6},{14,8},{16,10},{18,... | collective-permute-start | bytes 393224 | tf_op jit(solution)/shard_map/ppermute | solution.py:15
  28.3 19.0 %collective-permute-start.4 = (f32[2,2,32,256]{3,2,1,0:T(8,128)S(1)}, f32[2,2,32,256]{3,2,1,0:T(8,128)S(1)}, u32[]{:S(2)}, u32[]{:S(2)}) collective-permute-start(f32[2,2,32,256]{3,2,1,0:T(8,128)S(1)} %broadcast_select_fusion.21), channel_id=1, source_target_pairs={{0,24},{2,26},{4,28},{6,30},{8,0},{10,2},{12,4},{14,6},{16,8},{18,... | collective-permute-start | bytes 393224 | tf_op jit(solution)/shard_map/ppermute | solution.py:15
  43.4 21.5 %collective-permute-start.6 = (f32[2,2,32,256]{3,2,1,0:T(8,128)}, f32[2,2,32,256]{3,2,1,0:T(8,128)S(1)}, u32[]{:S(2)}, u32[]{:S(2)}) collective-permute-start(f32[2,2,32,256]{3,2,1,0:T(8,128)} %broadcast_select_fusion.19), channel_id=1, source_target_pairs={{0,20},{2,22},{4,24},{6,26},{8,28},{10,30},{12,0},{14,2},{16,4},{1... | collective-permute-start | bytes 393224 | tf_op jit(solution)/shard_map/ppermute | solution.py:15
  45.7 19.3 %collective-permute-start.7 = (f32[2,2,32,256]{3,2,1,0:T(8,128)}, f32[2,2,32,256]{3,2,1,0:T(8,128)S(1)}, u32[]{:S(2)}, u32[]{:S(2)}) collective-permute-start(f32[2,2,32,256]{3,2,1,0:T(8,128)} %broadcast_select_fusion.18), channel_id=1, source_target_pairs={{0,2},{2,4},{4,6},{6,8},{8,10},{10,12},{12,14},{14,16},{16,18},{18... | collective-permute-start | bytes 393224 | tf_op jit(solution)/shard_map/ppermute | solution.py:15
  45.8 19.3 %collective-permute-start.8 = (f32[2,2,32,256]{3,2,1,0:T(8,128)}, f32[2,2,32,256]{3,2,1,0:T(8,128)S(1)}, u32[]{:S(2)}, u32[]{:S(2)}) collective-permute-start(f32[2,2,32,256]{3,2,1,0:T(8,128)} %broadcast_select_fusion.17), channel_id=1, source_target_pairs={{0,4},{2,6},{4,8},{6,10},{8,12},{10,14},{12,16},{14,18},{16,20},{1... | collective-permute-start | bytes 393224 | tf_op jit(solution)/shard_map/ppermute | solution.py:15
  47.4 17.7 %collective-permute-start.9 = (f32[2,2,32,256]{3,2,1,0:T(8,128)}, f32[2,2,32,256]{3,2,1,0:T(8,128)S(1)}, u32[]{:S(2)}, u32[]{:S(2)}) collective-permute-start(f32[2,2,32,256]{3,2,1,0:T(8,128)} %broadcast_select_fusion.16), channel_id=1, source_target_pairs={{0,6},{2,8},{4,10},{6,12},{8,14},{10,16},{12,18},{14,20},{16,22},{... | collective-permute-start | bytes 393224 | tf_op jit(solution)/shard_map/ppermute | solution.py:15
  50.1 15.0 %collective-permute-start.10 = (f32[2,2,32,256]{3,2,1,0:T(8,128)S(1)}, f32[2,2,32,256]{3,2,1,0:T(8,128)S(1)}, u32[]{:S(2)}, u32[]{:S(2)}) collective-permute-start(f32[2,2,32,256]{3,2,1,0:T(8,128)S(1)} %broadcast_select_fusion.15), channel_id=1, source_target_pairs={{0,8},{2,10},{4,12},{6,14},{8,16},{10,18},{12,20},{14,22},{16,24},... | collective-permute-start | bytes 393224 | tf_op jit(solution)/shard_map/ppermute | solution.py:15
  352.5 33.0 %collective-permute-start.13 = (f32[2,2,32,256]{3,2,1,0:T(8,128)}, f32[2,2,32,256]{3,2,1,0:T(8,128)S(1)}, u32[]{:S(2)}, u32[]{:S(2)}) collective-permute-start(f32[2,2,32,256]{3,2,1,0:T(8,128)} %get-tuple-element.287), channel_id=1, source_target_pairs={{0,16},{2,18},{4,20},{6,22},{8,24},{10,26},{12,28},{14,30},{16,0},... | collective-permute-start | bytes 393224 | tf_op jit(solution)/shard_map/ppermute | solution.py:15
  352.5 33.7 %collective-permute-start.14 = (f32[2,2,32,256]{3,2,1,0:T(8,128)}, f32[2,2,32,256]{3,2,1,0:T(8,128)S(1)}, u32[]{:S(2)}, u32[]{:S(2)}) collective-permute-start(f32[2,2,32,256]{3,2,1,0:T(8,128)} %get-tuple-element.286), channel_id=1, source_target_pairs={{0,2},{2,4},{4,6},{6,8},{8,10},{10,12},{12,14},{14,16},{16,18},{18... | collective-permute-start | bytes 393224 | tf_op jit(solution)/shard_map/ppermute | solution.py:15
  352.6 36.6 %collective-permute-start.15 = (f32[2,2,32,256]{3,2,1,0:T(8,128)S(1)}, f32[2,2,32,256]{3,2,1,0:T(8,128)S(1)}, u32[]{:S(2)}, u32[]{:S(2)}) collective-permute-start(f32[2,2,32,256]{3,2,1,0:T(8,128)S(1)} %get-tuple-element.285), channel_id=1, source_target_pairs={{0,4},{2,6},{4,8},{6,10},{8,12},{10,14},{12,16},{14,18},{16,20},{1... | collective-permute-start | bytes 393224 | tf_op jit(solution)/shard_map/ppermute | solution.py:15
  352.7 41.3 %collective-permute-start.16 = (f32[2,2,32,256]{3,2,1,0:T(8,128)S(1)}, f32[2,2,32,256]{3,2,1,0:T(8,128)S(1)}, u32[]{:S(2)}, u32[]{:S(2)}) collective-permute-start(f32[2,2,32,256]{3,2,1,0:T(8,128)S(1)} %get-tuple-element.284), channel_id=1, source_target_pairs={{0,6},{2,8},{4,10},{6,12},{8,14},{10,16},{12,18},{14,20},{16,22},{... | collective-permute-start | bytes 393224 | tf_op jit(solution)/shard_map/ppermute | solution.py:15
  352.8 43.4 %collective-permute-start.17 = (f32[2,2,32,256]{3,2,1,0:T(8,128)S(1)}, f32[2,2,32,256]{3,2,1,0:T(8,128)S(1)}, u32[]{:S(2)}, u32[]{:S(2)}) collective-permute-start(f32[2,2,32,256]{3,2,1,0:T(8,128)S(1)} %get-tuple-element.283), channel_id=1, source_target_pairs={{0,8},{2,10},{4,12},{6,14},{8,16},{10,18},{12,20},{14,22},{16,24},... | collective-permute-start | bytes 393224 | tf_op jit(solution)/shard_map/ppermute | solution.py:15
  385.5 484.0 %reduce-scatter.9.cloned.1.call-start = ((), (), s32[]{:S(2)}) async-start(), calls=%async_computation.3 | async-start | bytes 393216
  449.3 20.4 %collective-permute-start.26 = (f32[2,2,32,256]{3,2,1,0:T(8,128)S(1)}, f32[2,2,32,256]{3,2,1,0:T(8,128)S(1)}, u32[]{:S(2)}, u32[]{:S(2)}) collective-permute-start(f32[2,2,32,256]{3,2,1,0:T(8,128)S(1)} %broadcast_select_fusion.12), channel_id=1, source_target_pairs={{0,16},{2,18},{4,20},{6,22},{8,24},{10,26},{12,28},{14,30},{16,0},... | collective-permute-start | bytes 393224 | tf_op jit(solution)/shard_map/ppermute | solution.py:15
  463.0 22.7 %collective-permute-start.29 = (f32[2,2,32,256]{3,2,1,0:T(8,128)S(1)}, f32[2,2,32,256]{3,2,1,0:T(8,128)S(1)}, u32[]{:S(2)}, u32[]{:S(2)}) collective-permute-start(f32[2,2,32,256]{3,2,1,0:T(8,128)S(1)} %broadcast_select_fusion.9), channel_id=1, source_target_pairs={{0,26},{2,28},{4,30},{6,0},{8,2},{10,4},{12,6},{14,8},{16,10},{18,... | collective-permute-start | bytes 393224 | tf_op jit(solution)/shard_map/ppermute | solution.py:15
  468.0 18.3 %collective-permute-start.30 = (f32[2,2,32,256]{3,2,1,0:T(8,128)S(1)}, f32[2,2,32,256]{3,2,1,0:T(8,128)S(1)}, u32[]{:S(2)}, u32[]{:S(2)}) collective-permute-start(f32[2,2,32,256]{3,2,1,0:T(8,128)S(1)} %broadcast_select_fusion.8), channel_id=1, source_target_pairs={{0,24},{2,26},{4,28},{6,30},{8,0},{10,2},{12,4},{14,6},{16,8},{18,... | collective-permute-start | bytes 393224 | tf_op jit(solution)/shard_map/ppermute | solution.py:15
  469.8 17.2 %collective-permute-start.31 = (f32[2,2,32,256]{3,2,1,0:T(8,128)S(1)}, f32[2,2,32,256]{3,2,1,0:T(8,128)S(1)}, u32[]{:S(2)}, u32[]{:S(2)}) collective-permute-start(f32[2,2,32,256]{3,2,1,0:T(8,128)S(1)} %broadcast_select_fusion.7), channel_id=1, source_target_pairs={{0,22},{2,24},{4,26},{6,28},{8,30},{10,0},{12,2},{14,4},{16,6},{18... | collective-permute-start | bytes 393224 | tf_op jit(solution)/shard_map/ppermute | solution.py:15
  470.4 20.7 %collective-permute-start.32 = (f32[2,2,32,256]{3,2,1,0:T(8,128)S(1)}, f32[2,2,32,256]{3,2,1,0:T(8,128)S(1)}, u32[]{:S(2)}, u32[]{:S(2)}) collective-permute-start(f32[2,2,32,256]{3,2,1,0:T(8,128)S(1)} %broadcast_select_fusion.6), channel_id=1, source_target_pairs={{0,20},{2,22},{4,24},{6,26},{8,28},{10,30},{12,0},{14,2},{16,4},{1... | collective-permute-start | bytes 393224 | tf_op jit(solution)/shard_map/ppermute | solution.py:15
  474.9 17.0 %collective-permute-start.33 = (f32[2,2,32,256]{3,2,1,0:T(8,128)S(1)}, f32[2,2,32,256]{3,2,1,0:T(8,128)S(1)}, u32[]{:S(2)}, u32[]{:S(2)}) collective-permute-start(f32[2,2,32,256]{3,2,1,0:T(8,128)S(1)} %broadcast_select_fusion.5), channel_id=1, source_target_pairs={{0,2},{2,4},{4,6},{6,8},{8,10},{10,12},{12,14},{14,16},{16,18},{18... | collective-permute-start | bytes 393224 | tf_op jit(solution)/shard_map/ppermute | solution.py:15
  807.2 32.7 %collective-permute-start.39 = (f32[2,2,32,256]{3,2,1,0:T(8,128)}, f32[2,2,32,256]{3,2,1,0:T(8,128)S(1)}, u32[]{:S(2)}, u32[]{:S(2)}) collective-permute-start(f32[2,2,32,256]{3,2,1,0:T(8,128)} %get-tuple-element.274), channel_id=1, source_target_pairs={{0,16},{2,18},{4,20},{6,22},{8,24},{10,26},{12,28},{14,30},{16,0},... | collective-permute-start | bytes 393224 | tf_op jit(solution)/shard_map/ppermute | solution.py:15
  807.2 33.4 %collective-permute-start.40 = (f32[2,2,32,256]{3,2,1,0:T(8,128)}, f32[2,2,32,256]{3,2,1,0:T(8,128)S(1)}, u32[]{:S(2)}, u32[]{:S(2)}) collective-permute-start(f32[2,2,32,256]{3,2,1,0:T(8,128)} %get-tuple-element.273), channel_id=1, source_target_pairs={{0,2},{2,4},{4,6},{6,8},{8,10},{10,12},{12,14},{14,16},{16,18},{18... | collective-permute-start | bytes 393224 | tf_op jit(solution)/shard_map/ppermute | solution.py:15
  807.3 36.5 %collective-permute-start.41 = (f32[2,2,32,256]{3,2,1,0:T(8,128)}, f32[2,2,32,256]{3,2,1,0:T(8,128)S(1)}, u32[]{:S(2)}, u32[]{:S(2)}) collective-permute-start(f32[2,2,32,256]{3,2,1,0:T(8,128)} %get-tuple-element.272), channel_id=1, source_target_pairs={{0,4},{2,6},{4,8},{6,10},{8,12},{10,14},{12,16},{14,18},{16,20},{1... | collective-permute-start | bytes 393224 | tf_op jit(solution)/shard_map/ppermute | solution.py:15
  807.4 41.2 %collective-permute-start.42 = (f32[2,2,32,256]{3,2,1,0:T(8,128)}, f32[2,2,32,256]{3,2,1,0:T(8,128)S(1)}, u32[]{:S(2)}, u32[]{:S(2)}) collective-permute-start(f32[2,2,32,256]{3,2,1,0:T(8,128)} %get-tuple-element.271), channel_id=1, source_target_pairs={{0,6},{2,8},{4,10},{6,12},{8,14},{10,16},{12,18},{14,20},{16,22},{... | collective-permute-start | bytes 393224 | tf_op jit(solution)/shard_map/ppermute | solution.py:15
  807.4 43.3 %collective-permute-start.43 = (f32[2,2,32,256]{3,2,1,0:T(8,128)}, f32[2,2,32,256]{3,2,1,0:T(8,128)S(1)}, u32[]{:S(2)}, u32[]{:S(2)}) collective-permute-start(f32[2,2,32,256]{3,2,1,0:T(8,128)} %get-tuple-element.270), channel_id=1, source_target_pairs={{0,8},{2,10},{4,12},{6,14},{8,16},{10,18},{12,20},{14,22},{16,24},... | collective-permute-start | bytes 393224 | tf_op jit(solution)/shard_map/ppermute | solution.py:15
  848.6 17.5 %collective-permute-start.47 = (f32[2,2,32,256]{3,2,1,0:T(8,128)}, f32[2,2,32,256]{3,2,1,0:T(8,128)S(1)}, u32[]{:S(2)}, u32[]{:S(2)}) collective-permute-start(f32[2,2,32,256]{3,2,1,0:T(8,128)} %get-tuple-element.266), channel_id=1, source_target_pairs={{0,28},{2,30},{4,0},{6,2},{8,4},{10,6},{12,8},{14,10},{16,12},{18,... | collective-permute-start | bytes 393224 | tf_op jit(solution)/shard_map/ppermute | solution.py:15
  850.7 16.1 %collective-permute-start.48 = (f32[2,2,32,256]{3,2,1,0:T(8,128)}, f32[2,2,32,256]{3,2,1,0:T(8,128)S(1)}, u32[]{:S(2)}, u32[]{:S(2)}) collective-permute-start(f32[2,2,32,256]{3,2,1,0:T(8,128)} %get-tuple-element.265), channel_id=1, source_target_pairs={{0,26},{2,28},{4,30},{6,0},{8,2},{10,4},{12,6},{14,8},{16,10},{18,... | collective-permute-start | bytes 393224 | tf_op jit(solution)/shard_map/ppermute | solution.py:15
  851.9 15.5 %collective-permute-start.49 = (f32[2,2,32,256]{3,2,1,0:T(8,128)}, f32[2,2,32,256]{3,2,1,0:T(8,128)S(1)}, u32[]{:S(2)}, u32[]{:S(2)}) collective-permute-start(f32[2,2,32,256]{3,2,1,0:T(8,128)} %get-tuple-element.264), channel_id=1, source_target_pairs={{0,24},{2,26},{4,28},{6,30},{8,0},{10,2},{12,4},{14,6},{16,8},{18,... | collective-permute-start | bytes 393224 | tf_op jit(solution)/shard_map/ppermute | solution.py:15
  854.0 14.1 %collective-permute-start.50 = (f32[2,2,32,256]{3,2,1,0:T(8,128)S(1)}, f32[2,2,32,256]{3,2,1,0:T(8,128)S(1)}, u32[]{:S(2)}, u32[]{:S(2)}) collective-permute-start(f32[2,2,32,256]{3,2,1,0:T(8,128)S(1)} %get-tuple-element.263), channel_id=1, source_target_pairs={{0,22},{2,24},{4,26},{6,28},{8,30},{10,0},{12,2},{14,4},{16,6},{18... | collective-permute-start | bytes 393224 | tf_op jit(solution)/shard_map/ppermute | solution.py:15
  (59 other events, 900.1 us)
Sparse Core Ops, SparseCore 0:
  385.6 8.0 reduce-scatter.6
  840.1 8.1 reduce-scatter.8
where the time goes:
time: 911 us; the launch traced here: 902 us
  matrix products  274 us (30%)
  local copies, waits for them, and re-layouts  178 us (20%)
  other arithmetic  178 us (20%)
  loops' own time  113 us (12%)
  starting transfers between devices  108 us (12%)
  waiting for transfers between devices  24.7 us (3%)
  between operations  15.2 us (2%)
  blocking collectives  10.5 us (1%)
    another operation x2, loops' own time, local(): lax.fori_loop(0, alive_count, apply_block, (start_near, start_back))  113 us
    unnamed x132, local copies, waits for them, and re-layouts  113 us
    ppermute x52, starting transfers between devices, from_behind(): return lax.ppermute(value, axis, pairs)  108 us
    scatter x42, other arithmetic, apply_block(): given_back = given_back.at[block_index].set(backward)  76 us
    dot_general x45, matrix products, complex_rows(): jnp.einsum('km,lm->kl', stacked, matrix[1], precision=HIGHEST, preferred_...  73.9 us
    dot_general x45, matrix products, complex_rows(): jnp.einsum('km,lm->kl', stacked, matrix[0], precision=HIGHEST, preferred_...  73.8 us
    another operation x84, other arithmetic  60.4 us
    dot_general x42, matrix products, complex_cols(): jnp.einsum('kl,lm->km', stacked, matrix[1], precision=HIGHEST, preferred_...  59.8 us
  transfers between devices with their start and end apart: 54, of which 7 were waited for; matrix products, arithmetic and copies ran while one was open for 11% of the time, Pallas kernels for 0%

commit v1 on v0

v1 whole, which is shorter than its diff:
```python
import functools

import jax
import jax.numpy as jnp
from jax import lax
from jax.experimental import pallas as pl
from jax.experimental.pallas import tpu as pltpu
from jax.sharding import PartitionSpec as P

ITERS = 2
F32 = jnp.float32
BF16 = jnp.bfloat16
MIB = 1 << 20


def split_value(value):
    high = value.astype(BF16)
    low = (value - high.astype(F32)).astype(BF16)
    return high, low


def stacked_parts(real, imag):
    real_high, real_low = split_value(real)
    imag_high, imag_low = split_value(imag)
    with_real = jnp.concatenate((real_high, imag_high, real_low, imag_low), axis=0)
    with_imag = jnp.concatenate((-imag_high, real_high, -imag_low, real_low), axis=0)
    return with_real, with_imag


def dot_nt(left, right):
    return lax.dot_general(left, right, (((1,), (1,)), ((), ())), preferred_element_type=F32)


def dot_nn(left, right):
    return jnp.dot(left, right, preferred_element_type=F32)


def tmat_kernel(mine_ref, theirs_ref, tmat_ref, side_ref, exciting_ref, scattered_ref):
    particles, _, directions, width = mine_ref.shape
    half = width // 2
    start = pl.multiple_of(side_ref[0] * half, half)
    for row in range(particles):
        real = mine_ref[row, 0] + theirs_ref[row, 0]
        imag = mine_ref[row, 1] + theirs_ref[row, 1]
        with_real, with_imag = stacked_parts(real, imag)
        real_high, real_low = split_value(tmat_ref[row, 0])
        imag_high, imag_low = split_value(tmat_ref[row, 1])
        total = dot_nt(real_high, with_real) + dot_nt(imag_high, with_imag)
        rest = dot_nt(real_low, with_real[: 2 * directions])
        rest += dot_nt(imag_low, with_imag[: 2 * directions])
        out = total[:, : 2 * directions] + total[:, 2 * directions :] + rest
        out = out.T
        scattered_ref[row, 0] = out[:directions]
        scattered_ref[row, 1] = out[directions:]
        for part in range(2):
            window = (row, part, slice(None), pl.ds(start, half))
            exciting_ref[row, part] = mine_ref[window] + theirs_ref[window]


def apply_tmat(mine, theirs, tmat, side):
    particles, _, directions, width = mine.shape
    half_shape = jax.ShapeDtypeStruct((particles, 2, directions, width // 2), F32)
    vmem = pl.BlockSpec(memory_space=pltpu.VMEM)
    return pl.pallas_call(
        tmat_kernel,
        out_shape=(half_shape, half_shape),
        in_specs=[vmem, vmem, vmem, pl.BlockSpec(memory_space=pltpu.SMEM)],
        out_specs=(vmem, vmem),
        compiler_params=pltpu.CompilerParams(vmem_limit_bytes=24 * MIB),
        name="tmat_apply",
    )(mine, theirs, tmat, side)


def backward_kernel(rows_ref, live_ref, partner_ref, field_ref, block_ref, out_ref, left_ref):
    slot = pl.program_id(0)
    directions = field_ref.shape[2]

    @pl.when(slot == 0)
    def _():
        for row in range(field_ref.shape[0]):
            with_real, with_imag = stacked_parts(field_ref[row, 0], field_ref[row, 1])
            left_ref[row, 0] = with_real
            left_ref[row, 1] = with_imag
        out_ref[...] = jnp.zeros_like(out_ref)

    @pl.when(slot < live_ref[0])
    def _():
        holder = rows_ref[slot]
        real_high, real_low = split_value(block_ref[0, 0])
        imag_high, imag_low = split_value(block_ref[0, 1])
        total = dot_nn(left_ref[holder, 0], real_high) + dot_nn(left_ref[holder, 1], imag_high)
        rest = dot_nn(left_ref[holder, 0, : 2 * directions], real_low)
        rest += dot_nn(left_ref[holder, 1, : 2 * directions], imag_low)
        out = total[: 2 * directions] + total[2 * directions :] + rest
        partner = partner_ref[slot]
        out_ref[partner, 0] = out[:directions]
        out_ref[partner, 1] = out[directions:]


def slot_block(slot, rows_ref, live_ref, partner_ref):
    return (jnp.minimum(slot, live_ref[0] - 1), 0, 0, 0)


def backward(rows, live, partner_row, field_full, blocks, total_rows):
    slots, _, width, half = blocks.shape
    particles, _, directions, _ = field_full.shape
    grid_spec = pltpu.PrefetchScalarGridSpec(
        num_scalar_prefetch=3,
        grid=(slots,),
        in_specs=[
            pl.BlockSpec(field_full.shape, lambda slot, *refs: (0, 0, 0, 0)),
            pl.BlockSpec((1, 2, width, half), slot_block),
        ],
        out_specs=pl.BlockSpec(
            (total_rows, 2, directions, half), lambda slot, *refs: (0, 0, 0, 0)
        ),
        scratch_shapes=[pltpu.VMEM((particles, 2, 4 * directions, width), BF16)],
    )
    return pl.pallas_call(
        backward_kernel,
        grid_spec=grid_spec,
        out_shape=jax.ShapeDtypeStruct((total_rows, 2, directions, half), F32),
        compiler_params=pltpu.CompilerParams(
            vmem_limit_bytes=44 * MIB, dimension_semantics=("arbitrary",)
        ),
        cost_estimate=pl.CostEstimate(
            flops=slots * 16 * directions * width * half,
            bytes_accessed=blocks.size * 4,
            transcendentals=0,
        ),
        name="blocks_backward",
    )(rows, live, partner_row, field_full, blocks)


def forward_kernel(rows_ref, live_ref, partner_ref, field_ref, block_ref, out_ref, acc_ref):
    slot = pl.program_id(0)
    directions = field_ref.shape[2]

    @pl.when(slot == 0)
    def _():
        acc_ref[...] = jnp.zeros_like(acc_ref)

    @pl.when(slot < live_ref[0])
    def _():
        holder = rows_ref[slot]
        with_real, with_imag = stacked_parts(field_ref[0, 0], field_ref[0, 1])
        real_high, real_low = split_value(block_ref[0, 0])
        imag_high, imag_low = split_value(block_ref[0, 1])
        total = dot_nt(real_high, with_real) + dot_nt(imag_high, with_imag)
        total += dot_nt(real_low, with_real) + dot_nt(imag_low, with_imag)
        acc_ref[holder] += total

    @pl.when(slot == pl.num_programs(0) - 1)
    def _():
        for row in range(acc_ref.shape[0]):
            total = acc_ref[row]
            out = (total[:, : 2 * directions] + total[:, 2 * directions :]).T
            out_ref[row, 0] = out[:directions]
            out_ref[row, 1] = out[directions:]


def slot_field(slot, rows_ref, live_ref, partner_ref):
    return (partner_ref[jnp.minimum(slot, live_ref[0] - 1)], 0, 0, 0)


def forward(rows, live, partner_row, every_field, blocks, particles):
    slots, _, width, half = blocks.shape
    directions = every_field.shape[2]
    grid_spec = pltpu.PrefetchScalarGridSpec(
        num_scalar_prefetch=3,
        grid=(slots,),
        in_specs=[
            pl.BlockSpec((1, 2, directions, half), slot_field),
            pl.BlockSpec((1, 2, width, half), slot_block),
        ],
        out_specs=pl.BlockSpec(
            (particles, 2, directions, width), lambda slot, *refs: (0, 0, 0, 0)
        ),
        scratch_shapes=[pltpu.VMEM((particles, width, 4 * directions), F32)],
    )
    return pl.pallas_call(
        forward_kernel,
        grid_spec=grid_spec,
        out_shape=jax.ShapeDtypeStruct((particles, 2, directions, width), F32),
        compiler_params=pltpu.CompilerParams(
            vmem_limit_bytes=24 * MIB, dimension_semantics=("arbitrary",)
        ),
        cost_estimate=pl.CostEstimate(
            flops=slots * 16 * directions * width * half,
            bytes_accessed=blocks.size * 4,
            transcendentals=0,
        ),
        name="blocks_forward",
    )(rows, live, partner_row, every_field, blocks)


def from_other(value):
    return lax.ppermute(value, "pair", [(0, 1), (1, 0)])


def local(incident, tmat, blocks, block_rows, partners, live, owner_of):
    particles, _, directions, half = incident.shape
    slots = blocks.shape[0]
    my_owner = lax.axis_index("owner")
    side = lax.axis_index("pair").astype(jnp.int32)
    my_partners = lax.dynamic_slice_in_dim(partners, my_owner * slots, slots)
    ids = jnp.arange(owner_of.shape[0], dtype=jnp.int32)
    partner_row = jnp.sum(
        jnp.where(my_partners[:, None] == ids[None, :], owner_of[None, :], 0), axis=1
    )
    total_rows = owner_of.shape[0]
    side_ref = side[None]

    def widened(value):
        zero = jnp.zeros_like(value)
        left = jnp.where(side == 0, value, zero)
        right = jnp.where(side == 1, value, zero)
        return jnp.concatenate((left, right), axis=3)

    mine = widened(incident)
    theirs = from_other(mine)
    exciting, scattered = apply_tmat(mine, theirs, tmat, side_ref)
    for _ in range(ITERS):
        every_field = lax.all_gather(scattered, "owner", axis=0, tiled=True)
        full = lax.all_gather(scattered, "pair", axis=3, tiled=True)
        given_back = backward(block_rows, live, partner_row, full, blocks, total_rows)
        returned = lax.psum_scatter(given_back, "owner", scatter_dimension=0, tiled=True)
        near = forward(block_rows, live, partner_row, every_field, blocks, particles)
        mine = near + widened(incident + returned)
        theirs = from_other(mine)
        exciting, scattered = apply_tmat(mine, theirs, tmat, side_ref)
    return (scattered, exciting)


def solution(mesh):
    in_specs = (
        P("owner", None, None, "pair"),
        P("owner", None, "pair", None),
        P("owner", None, None, "pair"),
        P("owner"),
        P(),
        P("owner"),
        P(),
    )
    out_specs = (P("owner", None, None, "pair"), P("owner", None, None, "pair"))
    return jax.shard_map(local, mesh=mesh, in_specs=in_specs, out_specs=out_specs, check_vma=False)
```

time: 911 us -> 313 us (0.34)
  matrix products: 274 us -> 0 us
  waiting for transfers between devices: 24.7 us -> 245 us
  other arithmetic: 178 us -> 3.04 us
  local copies, waits for them, and re-layouts: 178 us -> 21.5 us
  loops' own time: 113 us -> 0 us
  starting transfers between devices: 108 us -> 0.82 us
  Pallas kernels: 0 us -> 22 us
    dot_general x176 -> x0, matrix products: 274 us -> none  [the longest x45 73.9 us: complex_rows(): jnp.einsum('km,lm->kl', stacked, matrix[1], precision=HIGHEST, preferred_...]
    reduce_scatter x0 -> x2, waiting for transfers between devices: none -> 138 us  [local(): lax.psum_scatter(given_back, 'owner', scatter_dimension=0, tiled=True)]
    another operation x2 -> x0, loops' own time: 113 us -> none  [local(): lax.fori_loop(0, alive_count, apply_block, (start_near, start_back))]
    ppermute x52 -> x3, starting transfers between devices: 108 us -> 0.66 us  [from_other(): return lax.ppermute(value, 'pair', [(0, 1), (1, 0)])]
    all_gather x0 -> x2, waiting for transfers between devices: none -> 103 us  [local(): every_field = lax.all_gather(scattered, 'owner', axis=0, tiled=True)]
    unnamed x132 -> x20, local copies, waits for them, and re-layouts: 113 us -> 20.8 us
    scatter x42 -> x0, other arithmetic: 76 us -> none  [apply_block(): given_back = given_back.at[block_index].set(backward)]
    another operation x172 -> x0, other arithmetic: 62 us -> none
  transfers between devices with their start and end apart: 54 -> 7, of which waited for: 7 -> 7; matrix products, arithmetic and copies ran while one was open for 11% -> 0% of each run, Pallas kernels for 0% -> 6%
where the time goes in v1:
time: 313 us; the launch traced here: 312 us
  waiting for transfers between devices  245 us (78%)
  Pallas kernels  22 us (7%)
  local copies, waits for them, and re-layouts  21.5 us (7%)
  between operations  14.5 us (5%)
  blocking collectives  4.62 us (1%)
    reduce_scatter x2, waiting for transfers between devices, local(): lax.psum_scatter(given_back, 'owner', scatter_dimension=0, tiled=True)  138 us
    all_gather x2, waiting for transfers between devices, local(): every_field = lax.all_gather(scattered, 'owner', axis=0, tiled=True)  103 us
    unnamed x20, local copies, waits for them, and re-layouts  20.8 us
    pallas_call x2, Pallas kernels, backward(): pl.pallas_call(backward_kernel, grid_spec=grid_spec, out_shape=jax.ShapeD...  10.9 us
    pallas_call x2, Pallas kernels, forward(): pl.pallas_call(forward_kernel, grid_spec=grid_spec, out_shape=jax.ShapeDt...  6.69 us
  transfers between devices with their start and end apart: 7, of which 7 were waited for; matrix products, arithmetic and copies ran while one was open for 0% of the time, Pallas kernels for 6%

profile of v1, /device:TPU:0, one launch (start us, length us, event | category | flops | bytes accessed | tf_op | source)
XLA Modules:
  0.0 312.1 jit_solution(8992343192701728122)
XLA Ops:
  7.2 0.9 broadcast_select_fusion.5
  8.2 0.5 collective-permute-start
  8.7 1.2 collective-permute-done.theirs_ref
  9.9 1.6 copy-done.2
  11.5 1.5 tmat_apply.3
  13.0 0.0 reduce-scatter.3.cloned.1.call-start
  13.7 0.8 dynamic_slice.3
  14.4 0.2 select_reduce_fusion.partner_ref
  14.6 2.3 all_gather.13.field_ref
  16.9 6.1 %blocks_backward.2 = f32[32,2,32,256]{3,2,1,0:T(8,128)} custom-call(s32[21]{0:T(128)S(1)} %copy-done.7, s32[1]{0:T(128)S(6)} %copy.9.live_ref, s32[21]{0:T(128)S(1)} %select_reduce_fusion.partner_ref, f32[2,2,32,512]{3,2,1,0:T(8,128)S(1)} %all_gather.13.field_ref, f32[21,2,512,256]{3,2,1,0:T(8,128)} %block_ref.7), custom_call_target="tpu_custom_call" | custom-call | flops 1409286144 | bytes 22020096 | tf_op jit(solution)/shard_map/blocks_backward/pallas_call | solution.py:119
  23.1 53.4 %all-gather.3.cloned.1.call-done.field_ref = f32[32,2,32,256]{3,2,1,0:T(8,128)} async-done(((f32[2,2,32,256]{3,2,1,0:T(8,128)}), f32[32,2,32,256]{3,2,1,0:T(8,128)}) %all-gather.3.cloned.1.call-update) | async-done | bytes 2097168 | tf_op jit(solution)/shard_map/all_gather | solution.py:224
  76.5 7.3 %copy-done = f32[21,2,512,256]{3,2,1,0:T(8,128)S(1)} copy-done((f32[21,2,512,256]{3,2,1,0:T(8,128)S(1)}, f32[21,2,512,256]{3,2,1,0:T(8,128)}, u32[]{:S(2)}) %copy-start) | copy-done | bytes 22020120
  83.9 1.6 copy-done.5
  85.5 3.3 %blocks_forward.2 = f32[2,2,32,512]{3,2,1,0:T(8,128)S(1)} custom-call(s32[21]{0:T(128)S(1)} %copy-done.7, s32[1]{0:T(128)S(6)} %copy.9.live_ref, s32[21]{0:T(128)S(1)} %select_reduce_fusion.partner_ref, f32[32,2,32,256]{3,2,1,0:T(8,128)S(1)} %copy-done.5, f32[21,2,512,256]{3,2,1,0:T(8,128)S(1)} %copy-done), custom_call_target="tpu_custom_call" | custom-call | flops 1409286144 | bytes 22020096 | tf_op jit(solution)/shard_map/blocks_forward/pallas_call | solution.py:181
  88.8 69.2 %reduce-scatter.3.cloned.1.call-done = f32[2,2,32,256]{3,2,1,0:T(8,128)} async-done(((f32[32,2,32,256]{3,2,1,0:T(8,128)}), f32[2,2,32,256]{3,2,1,0:T(8,128)}) %reduce-scatter.3.cloned.1.call-update) | async-done | bytes 131088 | tf_op jit(solution)/shard_map/reduce_scatter | solution.py:227
  158.0 0.9 broadcast_select_fusion.3
  159.0 0.1 collective-permute-start.1
  159.1 1.5 collective-permute-done.1.theirs_ref
  160.6 1.5 tmat_apply.4
  162.1 0.0 reduce-scatter.5.cloned.1.call-start
  162.2 2.3 all_gather.15.field_ref
  164.5 4.8 %blocks_backward.3 = f32[32,2,32,256]{3,2,1,0:T(8,128)S(1)} custom-call(s32[21]{0:T(128)S(1)} %copy-done.7, s32[1]{0:T(128)S(6)} %copy.9.live_ref, s32[21]{0:T(128)S(1)} %select_reduce_fusion.partner_ref, f32[2,2,32,512]{3,2,1,0:T(8,128)S(1)} %all_gather.15.field_ref, f32[21,2,512,256]{3,2,1,0:T(8,128)} %block_ref.7), custom_call_target="tpu_custom_call" | custom-call | flops 1409286144 | bytes 22020096 | tf_op jit(solution)/shard_map/blocks_backward/pallas_call | solution.py:119
  169.3 1.3 copy-done.4
  170.6 49.6 %all-gather.5.cloned.1.call-done.field_ref = f32[32,2,32,256]{3,2,1,0:T(8,128)} async-done(((f32[2,2,32,256]{3,2,1,0:T(8,128)}), f32[32,2,32,256]{3,2,1,0:T(8,128)}) %all-gather.5.cloned.1.call-update) | async-done | bytes 2097168 | tf_op jit(solution)/shard_map/all_gather | solution.py:224
  220.2 7.3 %copy-done.1 = f32[21,2,512,256]{3,2,1,0:T(8,128)S(1)} copy-done((f32[21,2,512,256]{3,2,1,0:T(8,128)S(1)}, f32[21,2,512,256]{3,2,1,0:T(8,128)}, u32[]{:S(2)}) %copy-start.1) | copy-done | bytes 22020120
  227.5 1.6 copy-done.6
  229.1 3.3 %blocks_forward.3 = f32[2,2,32,512]{3,2,1,0:T(8,128)S(1)} custom-call(s32[21]{0:T(128)S(1)} %copy-done.7, s32[1]{0:T(128)S(6)} %copy.9.live_ref, s32[21]{0:T(128)S(1)} %select_reduce_fusion.partner_ref, f32[32,2,32,256]{3,2,1,0:T(8,128)S(1)} %copy-done.6, f32[21,2,512,256]{3,2,1,0:T(8,128)S(1)} %copy-done.1), custom_call_target="tpu_custom_call" | custom-call | flops 1409286144 | bytes 22020096 | tf_op jit(solution)/shard_map/blocks_forward/pallas_call | solution.py:181
  232.4 69.0 %reduce-scatter.5.cloned.1.call-done = f32[2,2,32,256]{3,2,1,0:T(8,128)} async-done(((f32[32,2,32,256]{3,2,1,0:T(8,128)}), f32[2,2,32,256]{3,2,1,0:T(8,128)}) %reduce-scatter.5.cloned.1.call-update) | async-done | bytes 131088 | tf_op jit(solution)/shard_map/reduce_scatter | solution.py:227
  301.5 0.9 broadcast_select_fusion.1
  302.4 0.1 collective-permute-start.2
  302.5 1.5 collective-permute-done.2.theirs_ref
  304.0 1.5 tmat_apply.5
  (23 shorter events, 0.3 us)
Async XLA Ops:
  7.2 7.3 %copy-start.9 = (s32[32]{0:T(128)S(1)}, s32[32]{0:T(128)}, u32[]{:S(2)}) copy-start(s32[32]{0:T(128)} %param.13) | copy-start | bytes 388
  7.2 9.8 %copy-start.7 = (s32[21]{0:T(128)S(1)}, s32[21]{0:T(128)}, u32[]{:S(2)}) copy-start(s32[21]{0:T(128)} %rows_ref.7) | copy-start | bytes 256
  7.2 69.4 %all-gather.3.cloned.1.call-start = ((), (), s32[]{:S(2)}) async-start(), calls=%async_computation.2 | async-start | bytes 2228224 | tf_op jit(solution)/shard_map/all_gather | solution.py:224
  8.2 1.7 collective-permute-start
  9.9 1.6 copy-start.2
  13.0 145.1 %reduce-scatter.3.cloned.1.call-start = ((), (), s32[]{:S(2)}) async-start(), calls=%async_computation.3 | async-start | bytes 2228224 | tf_op jit(solution)/shard_map/reduce_scatter | solution.py:227
  23.0 135.0 %copy-start.8 = (f32[2,2,32,256]{3,2,1,0:T(8,128)S(1)}, f32[2,2,32,256]{3,2,1,0:T(8,128)}, u32[]{:S(2)}) copy-start(f32[2,2,32,256]{3,2,1,0:T(8,128)} %param.7) | copy-start | bytes 393220
  23.1 197.1 %all-gather.5.cloned.1.call-start = ((), (), s32[]{:S(2)}) async-start(), calls=%async_computation.4 | async-start | bytes 2228224 | tf_op jit(solution)/shard_map/all_gather | solution.py:224
  76.5 7.3 %copy-start = (f32[21,2,512,256]{3,2,1,0:T(8,128)S(1)}, f32[21,2,512,256]{3,2,1,0:T(8,128)}, u32[]{:S(2)}) copy-start(f32[21,2,512,256]{3,2,1,0:T(8,128)} %block_ref.7) | copy-start | bytes 66060292
  83.9 1.6 copy-start.5
  85.5 75.2 %copy-start.3 = (f32[2,2,256,512]{3,2,1,0:T(8,128)S(1)}, f32[2,2,256,512]{3,2,1,0:T(8,128)}, u32[]{:S(2)}) copy-start(f32[2,2,256,512]{3,2,1,0:T(8,128)} %tmat_ref.5) | copy-start | bytes 6291460
  159.0 1.6 collective-permute-start.1
  162.1 139.3 %reduce-scatter.5.cloned.1.call-start = ((), (), s32[]{:S(2)}) async-start(), calls=%async_computation.5 | async-start | bytes 2228224 | tf_op jit(solution)/shard_map/reduce_scatter | solution.py:227
  169.3 1.3 copy-start.4
  220.2 7.3 %copy-start.1 = (f32[21,2,512,256]{3,2,1,0:T(8,128)S(1)}, f32[21,2,512,256]{3,2,1,0:T(8,128)}, u32[]{:S(2)}) copy-start(f32[21,2,512,256]{3,2,1,0:T(8,128)} %block_ref.7) | copy-start | bytes 66060292
  227.5 1.6 copy-start.6
  302.4 1.6 collective-permute-start.2
Sparse Core Ops, SparseCore 0:
  13.1 63.3 all-gather.2
  78.8 79.1 reduce-scatter.2
  162.3 57.8 all-gather.4
  222.3 79.1 reduce-scatter.4

commit v2 on v1

--- a/solution.py
+++ b/solution.py
@@ -8,6 +8,7 @@
 from jax.sharding import PartitionSpec as P
 
 ITERS = 2
+COLUMNS = 4
 F32 = jnp.float32
 BF16 = jnp.bfloat16
 MIB = 1 << 20
@@ -71,17 +72,22 @@
     )(mine, theirs, tmat, side)
 
 
-def backward_kernel(rows_ref, live_ref, partner_ref, field_ref, block_ref, out_ref, left_ref):
+def backward_kernel(rows_ref, live_ref, place_ref, side_ref, own_ref, other_ref, block_ref, *refs):
+    out_refs, left_ref = refs[:-1], refs[-1]
     slot = pl.program_id(0)
-    directions = field_ref.shape[2]
+    directions, half = own_ref.shape[2], own_ref.shape[3]
+    layers = out_refs[0].shape[0]
 
     @pl.when(slot == 0)
     def _():
-        for row in range(field_ref.shape[0]):
-            with_real, with_imag = stacked_parts(field_ref[row, 0], field_ref[row, 1])
-            left_ref[row, 0] = with_real
-            left_ref[row, 1] = with_imag
-        out_ref[...] = jnp.zeros_like(out_ref)
+        for field_ref, side in ((own_ref, side_ref[0]), (other_ref, 1 - side_ref[0])):
+            columns = pl.ds(pl.multiple_of(side * half, half), half)
+            for row in range(field_ref.shape[0]):
+                with_real, with_imag = stacked_parts(field_ref[row, 0], field_ref[row, 1])
+                left_ref[row, 0, :, columns] = with_real
+                left_ref[row, 1, :, columns] = with_imag
+        for out_ref in out_refs:
+            out_ref[...] = jnp.zeros_like(out_ref)
 
     @pl.when(slot < live_ref[0])
     def _():
@@ -92,34 +98,41 @@
         rest = dot_nn(left_ref[holder, 0, : 2 * directions], real_low)
         rest += dot_nn(left_ref[holder, 1, : 2 * directions], imag_low)
         out = total[: 2 * directions] + total[2 * directions :] + rest
-        partner = partner_ref[slot]
-        out_ref[partner, 0] = out[:directions]
-        out_ref[partner, 1] = out[directions:]
-
-
-def slot_block(slot, rows_ref, live_ref, partner_ref):
+        place = place_ref[slot]
+        which, layer = place // layers, place % layers
+        for number, out_ref in enumerate(out_refs):
+
+            @pl.when(which == number)
+            def _():
+                out_ref[layer, 0] = out[:directions]
+                out_ref[layer, 1] = out[directions:]
+
+
+def slot_block(slot, rows_ref, live_ref, *refs):
     return (jnp.minimum(slot, live_ref[0] - 1), 0, 0, 0)
 
 
-def backward(rows, live, partner_row, field_full, blocks, total_rows):
+def backward(rows, live, place, side, own_half, other_half, blocks, layers):
     slots, _, width, half = blocks.shape
-    particles, _, directions, _ = field_full.shape
+    particles, _, directions, _ = own_half.shape
+    whole = pl.BlockSpec(own_half.shape, lambda slot, *refs: (0, 0, 0, 0))
+    count = COLUMNS * particles
+    shape = (layers, 2, directions, half)
     grid_spec = pltpu.PrefetchScalarGridSpec(
-        num_scalar_prefetch=3,
+        num_scalar_prefetch=4,
         grid=(slots,),
         in_specs=[
-            pl.BlockSpec(field_full.shape, lambda slot, *refs: (0, 0, 0, 0)),
+            whole,
+            whole,
             pl.BlockSpec((1, 2, width, half), slot_block),
         ],
-        out_specs=pl.BlockSpec(
-            (total_rows, 2, directions, half), lambda slot, *refs: (0, 0, 0, 0)
-        ),
+        out_specs=[pl.BlockSpec(shape, lambda slot, *refs: (0, 0, 0, 0))] * count,
         scratch_shapes=[pltpu.VMEM((particles, 2, 4 * directions, width), BF16)],
     )
     return pl.pallas_call(
         backward_kernel,
         grid_spec=grid_spec,
-        out_shape=jax.ShapeDtypeStruct((total_rows, 2, directions, half), F32),
+        out_shape=[jax.ShapeDtypeStruct(shape, F32)] * count,
         compiler_params=pltpu.CompilerParams(
             vmem_limit_bytes=44 * MIB, dimension_semantics=("arbitrary",)
         ),
@@ -129,21 +142,27 @@
             transcendentals=0,
         ),
         name="blocks_backward",
-    )(rows, live, partner_row, field_full, blocks)
-
-
-def forward_kernel(rows_ref, live_ref, partner_ref, field_ref, block_ref, out_ref, acc_ref):
+    )(rows, live, place, side, own_half, other_half, blocks)
+
+
+def forward_kernel(pieces, rows_ref, live_ref, place_ref, *refs):
+    field_refs = refs[: len(pieces)]
+    block_ref, out_ref, every_ref, acc_ref = refs[len(pieces) :]
     slot = pl.program_id(0)
-    directions = field_ref.shape[2]
+    directions = every_ref.shape[2]
 
     @pl.when(slot == 0)
     def _():
         acc_ref[...] = jnp.zeros_like(acc_ref)
+        for first, field_ref in zip(pieces, field_refs):
+            for row in range(field_ref.shape[0]):
+                every_ref[first + row] = field_ref[row]
 
     @pl.when(slot < live_ref[0])
     def _():
         holder = rows_ref[slot]
-        with_real, with_imag = stacked_parts(field_ref[0, 0], field_ref[0, 1])
+        place = place_ref[slot]
+        with_real, with_imag = stacked_parts(every_ref[place, 0], every_ref[place, 1])
         real_high, real_low = split_value(block_ref[0, 0])
         imag_high, imag_low = split_value(block_ref[0, 1])
         total = dot_nt(real_high, with_real) + dot_nt(imag_high, with_imag)
@@ -159,31 +178,31 @@
             out_ref[row, 1] = out[directions:]
 
 
-def slot_field(slot, rows_ref, live_ref, partner_ref):
-    return (partner_ref[jnp.minimum(slot, live_ref[0] - 1)], 0, 0, 0)
-
-
-def forward(rows, live, partner_row, every_field, blocks, particles):
+def forward(rows, live, place, fields, blocks, particles):
     slots, _, width, half = blocks.shape
-    directions = every_field.shape[2]
+    directions = fields[0][1].shape[2]
+    count = sum(value.shape[0] for _, value in fields)
     grid_spec = pltpu.PrefetchScalarGridSpec(
         num_scalar_prefetch=3,
         grid=(slots,),
         in_specs=[
-            pl.BlockSpec((1, 2, directions, half), slot_field),
-            pl.BlockSpec((1, 2, width, half), slot_block),
-        ],
+            pl.BlockSpec(value.shape, lambda slot, *refs: (0, 0, 0, 0)) for _, value in fields
+        ]
+        + [pl.BlockSpec((1, 2, width, half), slot_block)],
         out_specs=pl.BlockSpec(
             (particles, 2, directions, width), lambda slot, *refs: (0, 0, 0, 0)
         ),
-        scratch_shapes=[pltpu.VMEM((particles, width, 4 * directions), F32)],
+        scratch_shapes=[
+            pltpu.VMEM((count, 2, directions, half), F32),
+            pltpu.VMEM((particles, width, 4 * directions), F32),
+        ],
     )
     return pl.pallas_call(
-        forward_kernel,
+        functools.partial(forward_kernel, tuple(first for first, _ in fields)),
         grid_spec=grid_spec,
         out_shape=jax.ShapeDtypeStruct((particles, 2, directions, width), F32),
         compiler_params=pltpu.CompilerParams(
-            vmem_limit_bytes=24 * MIB, dimension_semantics=("arbitrary",)
+            vmem_limit_bytes=48 * MIB, dimension_semantics=("arbitrary",)
         ),
         cost_estimate=pl.CostEstimate(
             flops=slots * 16 * directions * width * half,
@@ -191,7 +210,75 @@
             transcendentals=0,
         ),
         name="blocks_forward",
-    )(rows, live, partner_row, every_field, blocks)
+    )(rows, live, place, *[value for _, value in fields], blocks)
+
+
+def across(value, bit):
+    count = lax.axis_size("owner")
+    return lax.ppermute(value, "owner", [(source, source ^ bit) for source in range(count)])
+
+
+def along(value, shift):
+    count = lax.axis_size("owner")
+    step = shift * COLUMNS
+    return lax.ppermute(
+        value, "owner", [(source, (source + step) % count) for source in range(count)]
+    )
+
+
+def gather_rows(own, layers):
+    particles = len(own)
+    split = (particles + 1) // 2
+    rest = range(1, layers)
+    first_x = [across(value, 1) for value in own]
+    first_y = [across(value, 2) for value in own]
+    shifted = [[along(value, -shift) for value in own] for shift in rest]
+    tails = [
+        jnp.concatenate([shifted[shift - 1][particle] for shift in rest], axis=0)
+        for particle in range(particles)
+    ]
+    first_d = [
+        across(first_x[particle], 2) if particle < split else across(first_y[particle], 1)
+        for particle in range(particles)
+    ]
+    tails_x = [across(value, 1) for value in tails]
+    tails_y = [across(value, 2) for value in tails]
+    tails_d = [
+        across(tails_x[particle], 2) if particle < split else across(tails_y[particle], 1)
+        for particle in range(particles)
+    ]
+    found = []
+    for column, (heads, ends) in enumerate(
+        ((own, tails), (first_x, tails_x), (first_y, tails_y), (first_d, tails_d))
+    ):
+        for particle in range(particles):
+            base = (column * particles + particle) * layers
+            found.append((base, heads[particle]))
+            found.append((base + 1, ends[particle]))
+    return found
+
+
+def sum_back(products, particles, layers):
+    split = (particles + 1) // 2
+    own, to_x, to_y, to_d = (
+        list(products[column * particles : (column + 1) * particles]) for column in range(COLUMNS)
+    )
+    for particle in range(particles):
+        if particle < split:
+            to_y[particle] = to_y[particle] + across(to_d[particle], 1)
+        else:
+            to_x[particle] = to_x[particle] + across(to_d[particle], 2)
+    from_x = [across(value, 1) for value in to_x]
+    from_y = [across(value, 2) for value in to_y]
+    sums = [
+        [own[particle][layer] + from_x[particle][layer] + from_y[particle][layer] for particle in range(particles)]
+        for layer in range(layers)
+    ]
+    total = sums[0]
+    for layer in range(1, layers):
+        arrived = along(jnp.stack(sums[layer]), layer)
+        total = [total[particle] + arrived[particle] for particle in range(particles)]
+    return jnp.stack(total)
 
 
 def from_other(value):
@@ -201,14 +288,18 @@
 def local(incident, tmat, blocks, block_rows, partners, live, owner_of):
     particles, _, directions, half = incident.shape
     slots = blocks.shape[0]
-    my_owner = lax.axis_index("owner")
+    layers = lax.axis_size("owner") // COLUMNS
+    my_owner = lax.axis_index("owner").astype(jnp.int32)
     side = lax.axis_index("pair").astype(jnp.int32)
     my_partners = lax.dynamic_slice_in_dim(partners, my_owner * slots, slots)
     ids = jnp.arange(owner_of.shape[0], dtype=jnp.int32)
     partner_row = jnp.sum(
         jnp.where(my_partners[:, None] == ids[None, :], owner_of[None, :], 0), axis=1
     )
-    total_rows = owner_of.shape[0]
+    partner_owner = partner_row // particles
+    column = (partner_owner % COLUMNS) ^ (my_owner % COLUMNS)
+    layer = (partner_owner // COLUMNS - my_owner // COLUMNS) % layers
+    place = (column * particles + partner_row % particles) * layers + layer
     side_ref = side[None]
 
     def widened(value):
@@ -221,11 +312,12 @@
     theirs = from_other(mine)
     exciting, scattered = apply_tmat(mine, theirs, tmat, side_ref)
     for _ in range(ITERS):
-        every_field = lax.all_gather(scattered, "owner", axis=0, tiled=True)
-        full = lax.all_gather(scattered, "pair", axis=3, tiled=True)
-        given_back = backward(block_rows, live, partner_row, full, blocks, total_rows)
-        returned = lax.psum_scatter(given_back, "owner", scatter_dimension=0, tiled=True)
-        near = forward(block_rows, live, partner_row, every_field, blocks, particles)
+        own = [scattered[particle : particle + 1] for particle in range(particles)]
+        other = from_other(scattered)
+        fields = gather_rows(own, layers)
+        products = backward(block_rows, live, place, side_ref, scattered, other, blocks, layers)
+        near = forward(block_rows, live, place, fields, blocks, particles)
+        returned = sum_back(products, particles, layers)
         mine = near + widened(incident + returned)
         theirs = from_other(mine)
         exciting, scattered = apply_tmat(mine, theirs, tmat, side_ref)

time: 313 us -> 193 us (0.62)
  waiting for transfers between devices: 245 us -> 39.7 us
  starting transfers between devices: 0.82 us -> 78.5 us
  Pallas kernels: 22 us -> 64.3 us
  local copies, waits for them, and re-layouts: 21.5 us -> 3.1 us
  between operations: 14.5 us -> 1.75 us
  blocking collectives: 4.62 us -> 0 us
    reduce_scatter x2 -> x0, waiting for transfers between devices: 138 us -> none  [local(): lax.psum_scatter(given_back, 'owner', scatter_dimension=0, tiled=True)]
    all_gather x2 -> x0, waiting for transfers between devices: 103 us -> none  [local(): every_field = lax.all_gather(scattered, 'owner', axis=0, tiled=True)]
    ppermute x0 -> x54, starting transfers between devices: none -> 77.7 us  [the longest x36 39.4 us: across(): lax.ppermute(value, 'owner', [(source, source ^ bit) for source in range(...]
    pallas_call x4, Pallas kernels: 17.6 us -> 60 us  [the longest x2 31.4 us: forward(): pl.pallas_call(functools.partial(forward_kernel, tuple((first for first,...]
    ppermute x0 -> x54, waiting for transfers between devices: none -> 36.7 us  [the longest x36 36.6 us: across(): lax.ppermute(value, 'owner', [(source, source ^ bit) for source in range(...]
    unnamed x20 -> x18, local copies, waits for them, and re-layouts: 20.8 us -> 2.3 us
    all_gather x2 -> x0, blocking collectives: 4.62 us -> none  [local(): full = lax.all_gather(scattered, 'pair', axis=3, tiled=True)]
  transfers between devices with their start and end apart: 7 -> 59, of which waited for: 7 -> 16; matrix products, arithmetic and copies ran while one was open for 0% -> 1% of each run, Pallas kernels for 6% -> 32%
where the time goes in v2:
time: 193 us; the launch traced here: 190 us
  starting transfers between devices  78.5 us (41%)
  Pallas kernels  64.3 us (33%)
  waiting for transfers between devices  39.7 us (21%)
  local copies, waits for them, and re-layouts  3.1 us (2%)
  other arithmetic  2.4 us (1%)
    ppermute x36, starting transfers between devices, across(): lax.ppermute(value, 'owner', [(source, source ^ bit) for source in range(...  39.4 us
    ppermute x18, starting transfers between devices, along(): lax.ppermute(value, 'owner', [(source, (source + step) % count) for sourc...  38.3 us
    ppermute x36, waiting for transfers between devices, across(): lax.ppermute(value, 'owner', [(source, source ^ bit) for source in range(...  36.6 us
    pallas_call x2, Pallas kernels, forward(): pl.pallas_call(functools.partial(forward_kernel, tuple((first for first,...  31.4 us
    pallas_call x2, Pallas kernels, backward(): pl.pallas_call(backward_kernel, grid_spec=grid_spec, out_shape=[jax.Shape...  28.6 us
    pallas_call x3, Pallas kernels, apply_tmat(): pl.pallas_call(tmat_kernel, out_shape=(half_shape, half_shape), in_specs=...  4.33 us
  transfers between devices with their start and end apart: 59, of which 16 were waited for; matrix products, arithmetic and copies ran while one was open for 1% of the time, Pallas kernels for 32%

profile of v2, /device:TPU:0, one launch (start us, length us, event | category | flops | bytes accessed | tf_op | source)
XLA Modules:
  0.0 189.8 jit_solution(13723333722988432236)
XLA Ops:
  7.5 5.1 %collective-permute-start.4 = (f32[1,2,32,256]{3,2,1,0:T(8,128)S(1)}, f32[1,2,32,256]{3,2,1,0:T(8,128)S(1)}, u32[]{:S(2)}, u32[]{:S(2)}) collective-permute-start(f32[1,2,32,256]{3,2,1,0:T(8,128)S(1)} %get-tuple-element.64.refs_2_), channel_id=1, source_target_pairs={{0,24},{2,26},{4,28},{6,30},{8,0},{10,2},{12,4},{14,6},{16,8},{18,... | collective-permute-start | bytes 196616 | tf_op jit(solution)/shard_map/ppermute | solution.py:224
  13.6 2.8 %collective-permute-start.1 = (f32[1,2,32,256]{3,2,1,0:T(8,128)S(1)}, f32[1,2,32,256]{3,2,1,0:T(8,128)S(1)}, u32[]{:S(2)}, u32[]{:S(2)}) collective-permute-start(f32[1,2,32,256]{3,2,1,0:T(8,128)S(1)} %get-tuple-element.65.refs_0_), channel_id=1, source_target_pairs={{0,24},{2,26},{4,28},{6,30},{8,0},{10,2},{12,4},{14,6},{16,8},{18,... | collective-permute-start | bytes 196616 | tf_op jit(solution)/shard_map/ppermute | solution.py:224
  18.2 14.3 %blocks_backward.2 = (f32[4,2,32,256]{3,2,1,0:T(8,128)S(1)}, f32[4,2,32,256]{3,2,1,0:T(8,128)S(1)}, f32[4,2,32,256]{3,2,1,0:T(8,128)S(1)}, f32[4,2,32,256]{3,2,1...) custom-call(s32[21]{0:T(128)S(1)} %copy-done.2, ...), custom_call_target="tpu_custom_call" | custom-call | flops 1409286144 | bytes 22020096 | tf_op jit(solution)/shard_map/blocks_backward/pallas_call | solution.py:132
  34.1 2.7 %collective-permute-start.3 = (f32[1,2,32,256]{3,2,1,0:T(8,128)S(1)}, f32[1,2,32,256]{3,2,1,0:T(8,128)S(1)}, u32[]{:S(2)}, u32[]{:S(2)}) collective-permute-start(f32[1,2,32,256]{3,2,1,0:T(8,128)S(1)} %get-tuple-element.65.refs_0_), channel_id=1, source_target_pairs={{0,8},{2,10},{4,12},{6,14},{8,16},{10,18},{12,20},{14,22},{16,24},... | collective-permute-start | bytes 196616 | tf_op jit(solution)/shard_map/ppermute | solution.py:224
  36.9 2.5 %collective-permute-done.21 = f32[4,2,32,256]{3,2,1,0:T(8,128)S(1)} collective-permute-done((f32[4,2,32,256]{3,2,1,0:T(8,128)S(1)}, f32[4,2,32,256]{3,2,1,0:T(8,128)S(1)}, u32[]{:S(2)}, u32[]{:S(2)}) %collective-permute-start.21) | collective-permute-done | bytes 262176 | tf_op jit(solution)/shard_map/ppermute | solution.py:218
  41.7 4.5 %collective-permute-done.23 = f32[4,2,32,256]{3,2,1,0:T(8,128)S(1)} collective-permute-done((f32[4,2,32,256]{3,2,1,0:T(8,128)S(1)}, f32[4,2,32,256]{3,2,1,0:T(8,128)S(1)}, u32[]{:S(2)}, u32[]{:S(2)}) %collective-permute-start.23) | collective-permute-done | bytes 262176 | tf_op jit(solution)/shard_map/ppermute | solution.py:218
  46.2 2.1 %collective-permute-start.24 = (f32[4,2,32,256]{3,2,1,0:T(8,128)S(1)}, f32[4,2,32,256]{3,2,1,0:T(8,128)S(1)}, u32[]{:S(2)}, u32[]{:S(2)}) collective-permute-start(f32[4,2,32,256]{3,2,1,0:T(8,128)S(1)} %add.242), channel_id=1, source_target_pairs={{0,2},{2,0},{4,6},{6,4},{8,10},{10,8},{12,14},{14,12},{16,18},{18,... | collective-permute-start | bytes 786440 | tf_op jit(solution)/shard_map/ppermute | solution.py:218
  48.3 2.1 %collective-permute-start.13 = (f32[1,2,32,256]{3,2,1,0:T(8,128)S(1)}, f32[1,2,32,256]{3,2,1,0:T(8,128)S(1)}, u32[]{:S(2)}, u32[]{:S(2)}) collective-permute-start(f32[1,2,32,256]{3,2,1,0:T(8,128)S(1)} %get-tuple-element.64.refs_2_), channel_id=1, source_target_pairs={{0,4},{2,6},{4,0},{6,2},{8,12},{10,14},{12,8},{14,10},{16,20},{18,... | collective-permute-start | bytes 196616 | tf_op jit(solution)/shard_map/ppermute | solution.py:218
  51.8 5.6 %collective-permute-done.25 = f32[4,2,32,256]{3,2,1,0:T(8,128)S(1)} collective-permute-done((f32[4,2,32,256]{3,2,1,0:T(8,128)S(1)}, f32[4,2,32,256]{3,2,1,0:T(8,128)S(1)}, u32[]{:S(2)}, u32[]{:S(2)}) %collective-permute-start.25) | collective-permute-done | bytes 262176 | tf_op jit(solution)/shard_map/ppermute | solution.py:218
  59.6 2.1 %collective-permute-start.10 = (f32[3,2,32,256]{3,2,1,0:T(8,128)S(1)}, f32[3,2,32,256]{3,2,1,0:T(8,128)S(1)}, u32[]{:S(2)}, u32[]{:S(2)}) collective-permute-start(f32[3,2,32,256]{3,2,1,0:T(8,128)S(1)} %constant_dynamic-update-slice_fusion.3.refs_3_), channel_id=1, source_target_pairs={{0,2},{2,0},{4,6},{6,4},{8,10},{10,8},{12,14},{14,12},{16,18},{18,... | collective-permute-start | bytes 589832 | tf_op jit(solution)/shard_map/ppermute | solution.py:218
  61.6 2.0 %collective-permute-start.12 = (f32[3,2,32,256]{3,2,1,0:T(8,128)S(1)}, f32[3,2,32,256]{3,2,1,0:T(8,128)S(1)}, u32[]{:S(2)}, u32[]{:S(2)}) collective-permute-start(f32[3,2,32,256]{3,2,1,0:T(8,128)S(1)} %constant_dynamic-update-slice_fusion.refs_1_), channel_id=1, source_target_pairs={{0,4},{2,6},{4,0},{6,2},{8,12},{10,14},{12,8},{14,10},{16,20},{18,... | collective-permute-start | bytes 589832 | tf_op jit(solution)/shard_map/ppermute | solution.py:218
  65.4 2.4 %collective-permute-start.15 = (f32[1,2,32,256]{3,2,1,0:T(8,128)S(1)}, f32[1,2,32,256]{3,2,1,0:T(8,128)S(1)}, u32[]{:S(2)}, u32[]{:S(2)}) collective-permute-start(f32[1,2,32,256]{3,2,1,0:T(8,128)S(1)} %collective-permute-done.7.refs_4_), channel_id=1, source_target_pairs={{0,4},{2,6},{4,0},{6,2},{8,12},{10,14},{12,8},{14,10},{16,20},{18,... | collective-permute-start | bytes 196616 | tf_op jit(solution)/shard_map/ppermute | solution.py:218
  70.0 2.1 %collective-permute-start.17 = (f32[1,2,32,256]{3,2,1,0:T(8,128)S(1)}, f32[1,2,32,256]{3,2,1,0:T(8,128)S(1)}, u32[]{:S(2)}, u32[]{:S(2)}) collective-permute-start(f32[1,2,32,256]{3,2,1,0:T(8,128)S(1)} %collective-permute-done.13.refs_10_), channel_id=1, source_target_pairs={{0,2},{2,0},{4,6},{6,4},{8,10},{10,8},{12,14},{14,12},{16,18},{18,... | collective-permute-start | bytes 196616 | tf_op jit(solution)/shard_map/ppermute | solution.py:218
  72.1 2.2 %collective-permute-done.17.refs_14_ = f32[1,2,32,256]{3,2,1,0:T(8,128)S(1)} collective-permute-done((f32[1,2,32,256]{3,2,1,0:T(8,128)S(1)}, f32[1,2,32,256]{3,2,1,0:T(8,128)S(1)}, u32[]{:S(2)}, u32[]{:S(2)}) %collective-permute-start.17) | collective-permute-done | bytes 65568 | tf_op jit(solution)/shard_map/ppermute | solution.py:218
  74.4 2.1 %collective-permute-start.26 = (f32[2,2,32,256]{3,2,1,0:T(8,128)S(1)}, f32[2,2,32,256]{3,2,1,0:T(8,128)S(1)}, u32[]{:S(2)}, u32[]{:S(2)}) collective-permute-start(f32[2,2,32,256]{3,2,1,0:T(8,128)S(1)} %pad_maximum_fusion.1), channel_id=1, source_target_pairs={{0,8},{2,10},{4,12},{6,14},{8,16},{10,18},{12,20},{14,22},{16,24},... | collective-permute-start | bytes 393224 | tf_op jit(solution)/shard_map/ppermute | solution.py:224
  76.4 3.1 %collective-permute-start.27 = (f32[2,2,32,256]{3,2,1,0:T(8,128)S(1)}, f32[2,2,32,256]{3,2,1,0:T(8,128)S(1)}, u32[]{:S(2)}, u32[]{:S(2)}) collective-permute-start(f32[2,2,32,256]{3,2,1,0:T(8,128)S(1)} %pad_maximum_fusion.2), channel_id=1, source_target_pairs={{0,16},{2,18},{4,20},{6,22},{8,24},{10,26},{12,28},{14,30},{16,0},... | collective-permute-start | bytes 393224 | tf_op jit(solution)/shard_map/ppermute | solution.py:224
  80.3 15.7 %blocks_forward.2 = f32[2,2,32,512]{3,2,1,0:T(8,128)S(1)} custom-call(s32[21]{0:T(128)S(1)} %copy-done.3, s32[1]{0:T(128)S(6)} %copy.17.live_ref, s32[21]{0:T(128)S(1)} %fusion.1.place_ref, f32[1,2,32,256]{3,2,1,0:T(8,128)S(1)} %get-tuple-element.65.refs_0_, f32[3,2,32,256]{3,2,1,0:T(8,128)S(1)} %constant_dynamic-update-slice_fusion.refs_1_, ...), custom_call_target="tpu_custom_call" | custom-call | flops 1409286144 | bytes 22020096 | tf_op jit(solution)/shard_map/blocks_forward/pallas_call | solution.py:200
  99.4 3.4 %collective-permute-start.33 = (f32[1,2,32,256]{3,2,1,0:T(8,128)S(1)}, f32[1,2,32,256]{3,2,1,0:T(8,128)S(1)}, u32[]{:S(2)}, u32[]{:S(2)}) collective-permute-start(f32[1,2,32,256]{3,2,1,0:T(8,128)S(1)} %get-tuple-element.62.refs_2_), channel_id=1, source_target_pairs={{0,24},{2,26},{4,28},{6,30},{8,0},{10,2},{12,4},{14,6},{16,8},{18,... | collective-permute-start | bytes 196616 | tf_op jit(solution)/shard_map/ppermute | solution.py:224
  102.8 3.7 %collective-permute-start.34 = (f32[1,2,32,256]{3,2,1,0:T(8,128)S(1)}, f32[1,2,32,256]{3,2,1,0:T(8,128)S(1)}, u32[]{:S(2)}, u32[]{:S(2)}) collective-permute-start(f32[1,2,32,256]{3,2,1,0:T(8,128)S(1)} %get-tuple-element.62.refs_2_), channel_id=1, source_target_pairs={{0,16},{2,18},{4,20},{6,22},{8,24},{10,26},{12,28},{14,30},{16,0},... | collective-permute-start | bytes 196616 | tf_op jit(solution)/shard_map/ppermute | solution.py:224
  106.5 3.8 %collective-permute-start.30 = (f32[1,2,32,256]{3,2,1,0:T(8,128)S(1)}, f32[1,2,32,256]{3,2,1,0:T(8,128)S(1)}, u32[]{:S(2)}, u32[]{:S(2)}) collective-permute-start(f32[1,2,32,256]{3,2,1,0:T(8,128)S(1)} %get-tuple-element.63.refs_0_), channel_id=1, source_target_pairs={{0,24},{2,26},{4,28},{6,30},{8,0},{10,2},{12,4},{14,6},{16,8},{18,... | collective-permute-start | bytes 196616 | tf_op jit(solution)/shard_map/ppermute | solution.py:224
  110.3 14.3 %blocks_backward.3 = (f32[4,2,32,256]{3,2,1,0:T(8,128)S(1)}, f32[4,2,32,256]{3,2,1,0:T(8,128)S(1)}, f32[4,2,32,256]{3,2,1,0:T(8,128)S(1)}, f32[4,2,32,256]{3,2,1...) custom-call(s32[21]{0:T(128)S(1)} %copy-done.3, ...), custom_call_target="tpu_custom_call" | custom-call | flops 1409286144 | bytes 22020096 | tf_op jit(solution)/shard_map/blocks_backward/pallas_call | solution.py:132
  124.7 4.7 %collective-permute-start.32 = (f32[1,2,32,256]{3,2,1,0:T(8,128)S(1)}, f32[1,2,32,256]{3,2,1,0:T(8,128)S(1)}, u32[]{:S(2)}, u32[]{:S(2)}) collective-permute-start(f32[1,2,32,256]{3,2,1,0:T(8,128)S(1)} %get-tuple-element.63.refs_0_), channel_id=1, source_target_pairs={{0,8},{2,10},{4,12},{6,14},{8,16},{10,18},{12,20},{14,22},{16,24},... | collective-permute-start | bytes 196616 | tf_op jit(solution)/shard_map/ppermute | solution.py:224
  129.6 2.6 %collective-permute-done.50 = f32[4,2,32,256]{3,2,1,0:T(8,128)S(1)} collective-permute-done((f32[4,2,32,256]{3,2,1,0:T(8,128)S(1)}, f32[4,2,32,256]{3,2,1,0:T(8,128)S(1)}, u32[]{:S(2)}, u32[]{:S(2)}) %collective-permute-start.50) | collective-permute-done | bytes 262176 | tf_op jit(solution)/shard_map/ppermute | solution.py:218
  134.4 4.4 %collective-permute-done.52 = f32[4,2,32,256]{3,2,1,0:T(8,128)S(1)} collective-permute-done((f32[4,2,32,256]{3,2,1,0:T(8,128)S(1)}, f32[4,2,32,256]{3,2,1,0:T(8,128)S(1)}, u32[]{:S(2)}, u32[]{:S(2)}) %collective-permute-start.52) | collective-permute-done | bytes 262176 | tf_op jit(solution)/shard_map/ppermute | solution.py:218
  138.9 2.1 %collective-permute-start.53 = (f32[4,2,32,256]{3,2,1,0:T(8,128)S(1)}, f32[4,2,32,256]{3,2,1,0:T(8,128)S(1)}, u32[]{:S(2)}, u32[]{:S(2)}) collective-permute-start(f32[4,2,32,256]{3,2,1,0:T(8,128)S(1)} %add.268), channel_id=1, source_target_pairs={{0,2},{2,0},{4,6},{6,4},{8,10},{10,8},{12,14},{14,12},{16,18},{18,... | collective-permute-start | bytes 786440 | tf_op jit(solution)/shard_map/ppermute | solution.py:218
  140.9 2.1 %collective-permute-start.42 = (f32[1,2,32,256]{3,2,1,0:T(8,128)S(1)}, f32[1,2,32,256]{3,2,1,0:T(8,128)S(1)}, u32[]{:S(2)}, u32[]{:S(2)}) collective-permute-start(f32[1,2,32,256]{3,2,1,0:T(8,128)S(1)} %get-tuple-element.62.refs_2_), channel_id=1, source_target_pairs={{0,4},{2,6},{4,0},{6,2},{8,12},{10,14},{12,8},{14,10},{16,20},{18,... | collective-permute-start | bytes 196616 | tf_op jit(solution)/shard_map/ppermute | solution.py:218
  146.5 2.2 %collective-permute-done.54 = f32[4,2,32,256]{3,2,1,0:T(8,128)S(1)} collective-permute-done((f32[4,2,32,256]{3,2,1,0:T(8,128)S(1)}, f32[4,2,32,256]{3,2,1,0:T(8,128)S(1)}, u32[]{:S(2)}, u32[]{:S(2)}) %collective-permute-start.54) | collective-permute-done | bytes 262176 | tf_op jit(solution)/shard_map/ppermute | solution.py:218
  150.7 2.1 %collective-permute-start.40 = (f32[1,2,32,256]{3,2,1,0:T(8,128)S(1)}, f32[1,2,32,256]{3,2,1,0:T(8,128)S(1)}, u32[]{:S(2)}, u32[]{:S(2)}) collective-permute-start(f32[1,2,32,256]{3,2,1,0:T(8,128)S(1)} %get-tuple-element.63.refs_0_), channel_id=1, source_target_pairs={{0,4},{2,6},{4,0},{6,2},{8,12},{10,14},{12,8},{14,10},{16,20},{18,... | collective-permute-start | bytes 196616 | tf_op jit(solution)/shard_map/ppermute | solution.py:218
  153.2 4.7 %collective-permute-done.40.refs_8_ = f32[1,2,32,256]{3,2,1,0:T(8,128)S(1)} collective-permute-done((f32[1,2,32,256]{3,2,1,0:T(8,128)S(1)}, f32[1,2,32,256]{3,2,1,0:T(8,128)S(1)}, u32[]{:S(2)}, u32[]{:S(2)}) %collective-permute-start.40) | collective-permute-done | bytes 65568 | tf_op jit(solution)/shard_map/ppermute | solution.py:218
  164.4 2.5 %collective-permute-done.46.refs_14_ = f32[1,2,32,256]{3,2,1,0:T(8,128)S(1)} collective-permute-done((f32[1,2,32,256]{3,2,1,0:T(8,128)S(1)}, f32[1,2,32,256]{3,2,1,0:T(8,128)S(1)}, u32[]{:S(2)}, u32[]{:S(2)}) %collective-permute-start.46) | collective-permute-done | bytes 65568 | tf_op jit(solution)/shard_map/ppermute | solution.py:218
  168.6 2.3 %collective-permute-start.57 = (f32[2,2,32,256]{3,2,1,0:T(8,128)S(1)}, f32[2,2,32,256]{3,2,1,0:T(8,128)S(1)}, u32[]{:S(2)}, u32[]{:S(2)}) collective-permute-start(f32[2,2,32,256]{3,2,1,0:T(8,128)S(1)} %pad_maximum_fusion.6), channel_id=1, source_target_pairs={{0,24},{2,26},{4,28},{6,30},{8,0},{10,2},{12,4},{14,6},{16,8},{18,... | collective-permute-start | bytes 393224 | tf_op jit(solution)/shard_map/ppermute | solution.py:224
  170.9 15.7 %blocks_forward.3 = f32[2,2,32,512]{3,2,1,0:T(8,128)S(1)} custom-call(s32[21]{0:T(128)S(1)} %copy-done.3, s32[1]{0:T(128)S(6)} %copy.17.live_ref, s32[21]{0:T(128)S(1)} %fusion.1.place_ref, f32[1,2,32,256]{3,2,1,0:T(8,128)S(1)} %get-tuple-element.63.refs_0_, f32[3,2,32,256]{3,2,1,0:T(8,128)S(1)} %constant_dynamic-update-slice_fusion.6.refs_1_, ...), custom_call_target="tpu_custom_call" | custom-call | flops 1409286144 | bytes 22020096 | tf_op jit(solution)/shard_map/blocks_forward/pallas_call | solution.py:200
  (142 shorter events, 44.2 us)
Async XLA Ops:
  7.5 25.0 %collective-permute-start.4 = (f32[1,2,32,256]{3,2,1,0:T(8,128)S(1)}, f32[1,2,32,256]{3,2,1,0:T(8,128)S(1)}, u32[]{:S(2)}, u32[]{:S(2)}) collective-permute-start(f32[1,2,32,256]{3,2,1,0:T(8,128)S(1)} %get-tuple-element.64.refs_2_), channel_id=1, source_target_pairs={{0,24},{2,26},{4,28},{6,30},{8,0},{10,2},{12,4},{14,6},{16,8},{18,... | collective-permute-start | bytes 196616 | tf_op jit(solution)/shard_map/ppermute | solution.py:224
  12.6 24.2 %collective-permute-start.5 = (f32[1,2,32,256]{3,2,1,0:T(8,128)S(1)}, f32[1,2,32,256]{3,2,1,0:T(8,128)S(1)}, u32[]{:S(2)}, u32[]{:S(2)}) collective-permute-start(f32[1,2,32,256]{3,2,1,0:T(8,128)S(1)} %get-tuple-element.64.refs_2_), channel_id=1, source_target_pairs={{0,16},{2,18},{4,20},{6,22},{8,24},{10,26},{12,28},{14,30},{16,0},... | collective-permute-start | bytes 196616 | tf_op jit(solution)/shard_map/ppermute | solution.py:224
  12.6 28.4 %collective-permute-start.6 = (f32[1,2,32,256]{3,2,1,0:T(8,128)S(1)}, f32[1,2,32,256]{3,2,1,0:T(8,128)S(1)}, u32[]{:S(2)}, u32[]{:S(2)}) collective-permute-start(f32[1,2,32,256]{3,2,1,0:T(8,128)S(1)} %get-tuple-element.64.refs_2_), channel_id=1, source_target_pairs={{0,8},{2,10},{4,12},{6,14},{8,16},{10,18},{12,20},{14,22},{16,24},... | collective-permute-start | bytes 196616 | tf_op jit(solution)/shard_map/ppermute | solution.py:224
  13.6 20.5 %collective-permute-start.1 = (f32[1,2,32,256]{3,2,1,0:T(8,128)S(1)}, f32[1,2,32,256]{3,2,1,0:T(8,128)S(1)}, u32[]{:S(2)}, u32[]{:S(2)}) collective-permute-start(f32[1,2,32,256]{3,2,1,0:T(8,128)S(1)} %get-tuple-element.65.refs_0_), channel_id=1, source_target_pairs={{0,24},{2,26},{4,28},{6,30},{8,0},{10,2},{12,4},{14,6},{16,8},{18,... | collective-permute-start | bytes 196616 | tf_op jit(solution)/shard_map/ppermute | solution.py:224
  16.4 24.7 %collective-permute-start.2 = (f32[1,2,32,256]{3,2,1,0:T(8,128)S(1)}, f32[1,2,32,256]{3,2,1,0:T(8,128)S(1)}, u32[]{:S(2)}, u32[]{:S(2)}) collective-permute-start(f32[1,2,32,256]{3,2,1,0:T(8,128)S(1)} %get-tuple-element.65.refs_0_), channel_id=1, source_target_pairs={{0,16},{2,18},{4,20},{6,22},{8,24},{10,26},{12,28},{14,30},{16,0},... | collective-permute-start | bytes 196616 | tf_op jit(solution)/shard_map/ppermute | solution.py:224
  34.1 12.1 %collective-permute-start.3 = (f32[1,2,32,256]{3,2,1,0:T(8,128)S(1)}, f32[1,2,32,256]{3,2,1,0:T(8,128)S(1)}, u32[]{:S(2)}, u32[]{:S(2)}) collective-permute-start(f32[1,2,32,256]{3,2,1,0:T(8,128)S(1)} %get-tuple-element.65.refs_0_), channel_id=1, source_target_pairs={{0,8},{2,10},{4,12},{6,14},{8,16},{10,18},{12,20},{14,22},{16,24},... | collective-permute-start | bytes 196616 | tf_op jit(solution)/shard_map/ppermute | solution.py:224
  41.1 18.3 %collective-permute-start.7 = (f32[1,2,32,256]{3,2,1,0:T(8,128)S(1)}, f32[1,2,32,256]{3,2,1,0:T(8,128)S(1)}, u32[]{:S(2)}, u32[]{:S(2)}) collective-permute-start(f32[1,2,32,256]{3,2,1,0:T(8,128)S(1)} %get-tuple-element.65.refs_0_), channel_id=1, source_target_pairs={{0,2},{2,0},{4,6},{6,4},{8,10},{10,8},{12,14},{14,12},{16,18},{18,... | collective-permute-start | bytes 196616 | tf_op jit(solution)/shard_map/ppermute | solution.py:218
  46.1 11.2 %collective-permute-start.25 = (f32[4,2,32,256]{3,2,1,0:T(8,128)S(1)}, f32[4,2,32,256]{3,2,1,0:T(8,128)S(1)}, u32[]{:S(2)}, u32[]{:S(2)}) collective-permute-start(f32[4,2,32,256]{3,2,1,0:T(8,128)S(1)} %get-tuple-element.30), channel_id=1, source_target_pairs={{0,4},{2,6},{4,0},{6,2},{8,12},{10,14},{12,8},{14,10},{16,20},{18,... | collective-permute-start | bytes 786440 | tf_op jit(solution)/shard_map/ppermute | solution.py:218
  46.2 11.2 %collective-permute-start.24 = (f32[4,2,32,256]{3,2,1,0:T(8,128)S(1)}, f32[4,2,32,256]{3,2,1,0:T(8,128)S(1)}, u32[]{:S(2)}, u32[]{:S(2)}) collective-permute-start(f32[4,2,32,256]{3,2,1,0:T(8,128)S(1)} %add.242), channel_id=1, source_target_pairs={{0,2},{2,0},{4,6},{6,4},{8,10},{10,8},{12,14},{14,12},{16,18},{18,... | collective-permute-start | bytes 786440 | tf_op jit(solution)/shard_map/ppermute | solution.py:218
  48.3 11.3 %collective-permute-start.13 = (f32[1,2,32,256]{3,2,1,0:T(8,128)S(1)}, f32[1,2,32,256]{3,2,1,0:T(8,128)S(1)}, u32[]{:S(2)}, u32[]{:S(2)}) collective-permute-start(f32[1,2,32,256]{3,2,1,0:T(8,128)S(1)} %get-tuple-element.64.refs_2_), channel_id=1, source_target_pairs={{0,4},{2,6},{4,0},{6,2},{8,12},{10,14},{12,8},{14,10},{16,20},{18,... | collective-permute-start | bytes 196616 | tf_op jit(solution)/shard_map/ppermute | solution.py:218
  57.4 11.8 %collective-permute-start.8 = (f32[3,2,32,256]{3,2,1,0:T(8,128)S(1)}, f32[3,2,32,256]{3,2,1,0:T(8,128)S(1)}, u32[]{:S(2)}, u32[]{:S(2)}) collective-permute-start(f32[3,2,32,256]{3,2,1,0:T(8,128)S(1)} %constant_dynamic-update-slice_fusion.refs_1_), channel_id=1, source_target_pairs={{0,2},{2,0},{4,6},{6,4},{8,10},{10,8},{12,14},{14,12},{16,18},{18,... | collective-permute-start | bytes 589832 | tf_op jit(solution)/shard_map/ppermute | solution.py:218
  59.6 16.9 %collective-permute-start.10 = (f32[3,2,32,256]{3,2,1,0:T(8,128)S(1)}, f32[3,2,32,256]{3,2,1,0:T(8,128)S(1)}, u32[]{:S(2)}, u32[]{:S(2)}) collective-permute-start(f32[3,2,32,256]{3,2,1,0:T(8,128)S(1)} %constant_dynamic-update-slice_fusion.3.refs_3_), channel_id=1, source_target_pairs={{0,2},{2,0},{4,6},{6,4},{8,10},{10,8},{12,14},{14,12},{16,18},{18,... | collective-permute-start | bytes 589832 | tf_op jit(solution)/shard_map/ppermute | solution.py:218
  61.6 17.9 %collective-permute-start.12 = (f32[3,2,32,256]{3,2,1,0:T(8,128)S(1)}, f32[3,2,32,256]{3,2,1,0:T(8,128)S(1)}, u32[]{:S(2)}, u32[]{:S(2)}) collective-permute-start(f32[3,2,32,256]{3,2,1,0:T(8,128)S(1)} %constant_dynamic-update-slice_fusion.refs_1_), channel_id=1, source_target_pairs={{0,4},{2,6},{4,0},{6,2},{8,12},{10,14},{12,8},{14,10},{16,20},{18,... | collective-permute-start | bytes 589832 | tf_op jit(solution)/shard_map/ppermute | solution.py:218
  67.8 12.5 %collective-permute-start.18 = (f32[3,2,32,256]{3,2,1,0:T(8,128)S(1)}, f32[3,2,32,256]{3,2,1,0:T(8,128)S(1)}, u32[]{:S(2)}, u32[]{:S(2)}) collective-permute-start(f32[3,2,32,256]{3,2,1,0:T(8,128)S(1)} %collective-permute-done.14.refs_11_), channel_id=1, source_target_pairs={{0,2},{2,0},{4,6},{6,4},{8,10},{10,8},{12,14},{14,12},{16,18},{18,... | collective-permute-start | bytes 589832 | tf_op jit(solution)/shard_map/ppermute | solution.py:218
  74.4 21.7 %collective-permute-start.26 = (f32[2,2,32,256]{3,2,1,0:T(8,128)S(1)}, f32[2,2,32,256]{3,2,1,0:T(8,128)S(1)}, u32[]{:S(2)}, u32[]{:S(2)}) collective-permute-start(f32[2,2,32,256]{3,2,1,0:T(8,128)S(1)} %pad_maximum_fusion.1), channel_id=1, source_target_pairs={{0,8},{2,10},{4,12},{6,14},{8,16},{10,18},{12,20},{14,22},{16,24},... | collective-permute-start | bytes 393224 | tf_op jit(solution)/shard_map/ppermute | solution.py:224
  76.4 19.6 %collective-permute-start.27 = (f32[2,2,32,256]{3,2,1,0:T(8,128)S(1)}, f32[2,2,32,256]{3,2,1,0:T(8,128)S(1)}, u32[]{:S(2)}, u32[]{:S(2)}) collective-permute-start(f32[2,2,32,256]{3,2,1,0:T(8,128)S(1)} %pad_maximum_fusion.2), channel_id=1, source_target_pairs={{0,16},{2,18},{4,20},{6,22},{8,24},{10,26},{12,28},{14,30},{16,0},... | collective-permute-start | bytes 393224 | tf_op jit(solution)/shard_map/ppermute | solution.py:224
  79.5 16.6 %collective-permute-start.28 = (f32[2,2,32,256]{3,2,1,0:T(8,128)S(1)}, f32[2,2,32,256]{3,2,1,0:T(8,128)S(1)}, u32[]{:S(2)}, u32[]{:S(2)}) collective-permute-start(f32[2,2,32,256]{3,2,1,0:T(8,128)S(1)} %pad_maximum_fusion.3), channel_id=1, source_target_pairs={{0,24},{2,26},{4,28},{6,30},{8,0},{10,2},{12,4},{14,6},{16,8},{18,... | collective-permute-start | bytes 393224 | tf_op jit(solution)/shard_map/ppermute | solution.py:224
  99.4 25.2 %collective-permute-start.33 = (f32[1,2,32,256]{3,2,1,0:T(8,128)S(1)}, f32[1,2,32,256]{3,2,1,0:T(8,128)S(1)}, u32[]{:S(2)}, u32[]{:S(2)}) collective-permute-start(f32[1,2,32,256]{3,2,1,0:T(8,128)S(1)} %get-tuple-element.62.refs_2_), channel_id=1, source_target_pairs={{0,24},{2,26},{4,28},{6,30},{8,0},{10,2},{12,4},{14,6},{16,8},{18,... | collective-permute-start | bytes 196616 | tf_op jit(solution)/shard_map/ppermute | solution.py:224
  102.8 26.7 %collective-permute-start.34 = (f32[1,2,32,256]{3,2,1,0:T(8,128)S(1)}, f32[1,2,32,256]{3,2,1,0:T(8,128)S(1)}, u32[]{:S(2)}, u32[]{:S(2)}) collective-permute-start(f32[1,2,32,256]{3,2,1,0:T(8,128)S(1)} %get-tuple-element.62.refs_2_), channel_id=1, source_target_pairs={{0,16},{2,18},{4,20},{6,22},{8,24},{10,26},{12,28},{14,30},{16,0},... | collective-permute-start | bytes 196616 | tf_op jit(solution)/shard_map/ppermute | solution.py:224
  106.5 26.0 %collective-permute-start.35 = (f32[1,2,32,256]{3,2,1,0:T(8,128)S(1)}, f32[1,2,32,256]{3,2,1,0:T(8,128)S(1)}, u32[]{:S(2)}, u32[]{:S(2)}) collective-permute-start(f32[1,2,32,256]{3,2,1,0:T(8,128)S(1)} %get-tuple-element.62.refs_2_), channel_id=1, source_target_pairs={{0,8},{2,10},{4,12},{6,14},{8,16},{10,18},{12,20},{14,22},{16,24},... | collective-permute-start | bytes 196616 | tf_op jit(solution)/shard_map/ppermute | solution.py:224
  106.5 18.2 %collective-permute-start.30 = (f32[1,2,32,256]{3,2,1,0:T(8,128)S(1)}, f32[1,2,32,256]{3,2,1,0:T(8,128)S(1)}, u32[]{:S(2)}, u32[]{:S(2)}) collective-permute-start(f32[1,2,32,256]{3,2,1,0:T(8,128)S(1)} %get-tuple-element.63.refs_0_), channel_id=1, source_target_pairs={{0,24},{2,26},{4,28},{6,30},{8,0},{10,2},{12,4},{14,6},{16,8},{18,... | collective-permute-start | bytes 196616 | tf_op jit(solution)/shard_map/ppermute | solution.py:224
  110.3 23.5 %collective-permute-start.31 = (f32[1,2,32,256]{3,2,1,0:T(8,128)S(1)}, f32[1,2,32,256]{3,2,1,0:T(8,128)S(1)}, u32[]{:S(2)}, u32[]{:S(2)}) collective-permute-start(f32[1,2,32,256]{3,2,1,0:T(8,128)S(1)} %get-tuple-element.63.refs_0_), channel_id=1, source_target_pairs={{0,16},{2,18},{4,20},{6,22},{8,24},{10,26},{12,28},{14,30},{16,0},... | collective-permute-start | bytes 196616 | tf_op jit(solution)/shard_map/ppermute | solution.py:224
  124.7 14.1 %collective-permute-start.32 = (f32[1,2,32,256]{3,2,1,0:T(8,128)S(1)}, f32[1,2,32,256]{3,2,1,0:T(8,128)S(1)}, u32[]{:S(2)}, u32[]{:S(2)}) collective-permute-start(f32[1,2,32,256]{3,2,1,0:T(8,128)S(1)} %get-tuple-element.63.refs_0_), channel_id=1, source_target_pairs={{0,8},{2,10},{4,12},{6,14},{8,16},{10,18},{12,20},{14,22},{16,24},... | collective-permute-start | bytes 196616 | tf_op jit(solution)/shard_map/ppermute | solution.py:224
  132.5 11.9 %collective-permute-start.51 = (f32[4,2,32,256]{3,2,1,0:T(8,128)S(1)}, f32[4,2,32,256]{3,2,1,0:T(8,128)S(1)}, u32[]{:S(2)}, u32[]{:S(2)}) collective-permute-start(f32[4,2,32,256]{3,2,1,0:T(8,128)S(1)} %add.264), channel_id=1, source_target_pairs={{0,4},{2,6},{4,0},{6,2},{8,12},{10,14},{12,8},{14,10},{16,20},{18,... | collective-permute-start | bytes 786440 | tf_op jit(solution)/shard_map/ppermute | solution.py:218
  133.8 16.9 %collective-permute-start.36 = (f32[1,2,32,256]{3,2,1,0:T(8,128)S(1)}, f32[1,2,32,256]{3,2,1,0:T(8,128)S(1)}, u32[]{:S(2)}, u32[]{:S(2)}) collective-permute-start(f32[1,2,32,256]{3,2,1,0:T(8,128)S(1)} %get-tuple-element.63.refs_0_), channel_id=1, source_target_pairs={{0,2},{2,0},{4,6},{6,4},{8,10},{10,8},{12,14},{14,12},{16,18},{18,... | collective-permute-start | bytes 196616 | tf_op jit(solution)/shard_map/ppermute | solution.py:218
  140.9 11.9 %collective-permute-start.42 = (f32[1,2,32,256]{3,2,1,0:T(8,128)S(1)}, f32[1,2,32,256]{3,2,1,0:T(8,128)S(1)}, u32[]{:S(2)}, u32[]{:S(2)}) collective-permute-start(f32[1,2,32,256]{3,2,1,0:T(8,128)S(1)} %get-tuple-element.62.refs_2_), channel_id=1, source_target_pairs={{0,4},{2,6},{4,0},{6,2},{8,12},{10,14},{12,8},{14,10},{16,20},{18,... | collective-permute-start | bytes 196616 | tf_op jit(solution)/shard_map/ppermute | solution.py:218
  152.8 15.7 %collective-permute-start.39 = (f32[3,2,32,256]{3,2,1,0:T(8,128)S(1)}, f32[3,2,32,256]{3,2,1,0:T(8,128)S(1)}, u32[]{:S(2)}, u32[]{:S(2)}) collective-permute-start(f32[3,2,32,256]{3,2,1,0:T(8,128)S(1)} %constant_dynamic-update-slice_fusion.9.refs_3_), channel_id=1, source_target_pairs={{0,2},{2,0},{4,6},{6,4},{8,10},{10,8},{12,14},{14,12},{16,18},{18,... | collective-permute-start | bytes 589832 | tf_op jit(solution)/shard_map/ppermute | solution.py:218
  152.9 15.6 %collective-permute-start.41 = (f32[3,2,32,256]{3,2,1,0:T(8,128)S(1)}, f32[3,2,32,256]{3,2,1,0:T(8,128)S(1)}, u32[]{:S(2)}, u32[]{:S(2)}) collective-permute-start(f32[3,2,32,256]{3,2,1,0:T(8,128)S(1)} %constant_dynamic-update-slice_fusion.6.refs_1_), channel_id=1, source_target_pairs={{0,4},{2,6},{4,0},{6,2},{8,12},{10,14},{12,8},{14,10},{16,20},{18,... | collective-permute-start | bytes 589832 | tf_op jit(solution)/shard_map/ppermute | solution.py:218
  158.2 12.7 %collective-permute-start.47 = (f32[3,2,32,256]{3,2,1,0:T(8,128)S(1)}, f32[3,2,32,256]{3,2,1,0:T(8,128)S(1)}, u32[]{:S(2)}, u32[]{:S(2)}) collective-permute-start(f32[3,2,32,256]{3,2,1,0:T(8,128)S(1)} %collective-permute-done.43.refs_11_), channel_id=1, source_target_pairs={{0,2},{2,0},{4,6},{6,4},{8,10},{10,8},{12,14},{14,12},{16,18},{18,... | collective-permute-start | bytes 589832 | tf_op jit(solution)/shard_map/ppermute | solution.py:218
  167.0 19.6 %collective-permute-start.55 = (f32[2,2,32,256]{3,2,1,0:T(8,128)S(1)}, f32[2,2,32,256]{3,2,1,0:T(8,128)S(1)}, u32[]{:S(2)}, u32[]{:S(2)}) collective-permute-start(f32[2,2,32,256]{3,2,1,0:T(8,128)S(1)} %pad_maximum_fusion.4), channel_id=1, source_target_pairs={{0,8},{2,10},{4,12},{6,14},{8,16},{10,18},{12,20},{14,22},{16,24},... | collective-permute-start | bytes 393224 | tf_op jit(solution)/shard_map/ppermute | solution.py:224
  168.5 18.1 %collective-permute-start.56 = (f32[2,2,32,256]{3,2,1,0:T(8,128)S(1)}, f32[2,2,32,256]{3,2,1,0:T(8,128)S(1)}, u32[]{:S(2)}, u32[]{:S(2)}) collective-permute-start(f32[2,2,32,256]{3,2,1,0:T(8,128)S(1)} %pad_maximum_fusion.5), channel_id=1, source_target_pairs={{0,16},{2,18},{4,20},{6,22},{8,24},{10,26},{12,28},{14,30},{16,0},... | collective-permute-start | bytes 393224 | tf_op jit(solution)/shard_map/ppermute | solution.py:224
  168.6 18.0 %collective-permute-start.57 = (f32[2,2,32,256]{3,2,1,0:T(8,128)S(1)}, f32[2,2,32,256]{3,2,1,0:T(8,128)S(1)}, u32[]{:S(2)}, u32[]{:S(2)}) collective-permute-start(f32[2,2,32,256]{3,2,1,0:T(8,128)S(1)} %pad_maximum_fusion.6), channel_id=1, source_target_pairs={{0,24},{2,26},{4,28},{6,30},{8,0},{10,2},{12,4},{14,6},{16,8},{18,... | collective-permute-start | bytes 393224 | tf_op jit(solution)/shard_map/ppermute | solution.py:224
  (32 other events, 454.0 us)
